TPU v7x, 256 devices: a whole 4x4x8 slice. The times are simulated.
256 devices in a mesh: pipe: 8 (over z_lo, core), expert: 32 (over y, z_hi, x).
Axes of the slice: x: 4, y: 4, z: 8 (z_hi: 2, z_lo: 4; z = z_hi * 4 + z_lo), core: 2. Of those that a mesh axis runs over, the one named last changes fastest.
Arguments:
- tokens: bfloat16 [32768, 7168], P(('pipe', 'expert')), may hold values from -6 to 6
- cotangent: bfloat16 [32768, 7168], P(('pipe', 'expert')), may hold values from -6 to 6
- expert_ids: int32 [32768, 8], P(('pipe', 'expert')), may hold values from 0 to 255, all different within a row; in each aligned block of 128 rows (0 to 127, 128 to 255, ...) at most 8 rows name the same one
- gate_weights: float32 [32768, 8], P(('pipe', 'expert')), may hold values from 0.1 to 0.6
- w_gate: bfloat16 [8, 3584, 4096], P('pipe', None, 'expert'), may hold values from -0.0625 to 0.0625
- w_up: bfloat16 [8, 3584, 4096], P('pipe', None, 'expert'), may hold values from -0.0625 to 0.0625
- w_down: bfloat16 [8, 4096, 3584], P('pipe', 'expert'), may hold values from -0.1875 to 0.1875
Outputs:
- mixed_out: bfloat16 [32768, 7168], P(('pipe', 'expert'))
- input_grad: bfloat16 [32768, 7168], P(('pipe', 'expert'))
- grad_gate: bfloat16 [8, 3584, 4096], P('pipe', None, 'expert')
- grad_up: bfloat16 [8, 3584, 4096], P('pipe', None, 'expert')
- grad_down: bfloat16 [8, 4096, 3584], P('pipe', 'expert')
Inputs may be any that keep to these rules, and one draw needn't show every extreme that they name: `expert_ids`: the 8 entries of a row differ. In each block of 128 rows, no expert is named more than 8 times, a bound that some block reaches.
All inputs are finite; a program needn't handle non-finite values.
Results may differ from a plain program's by a relative error of at most 0.0065.
Values may be sent and summed in bfloat16 or wider, within the bound.
A program may use at most 128 MiB of HBM per device.

v0:
```python
import jax
import jax.numpy as jnp
from jax import lax
from jax.sharding import PartitionSpec as P

GROUP = 8
CAP = 8


def swapped(block, axis, stride):
    count = lax.axis_size(axis)
    route = []
    for low in range(count):
        high = low | 1 << stride
        if high != low and high < count:
            route += [(low, high), (high, low)]
    return lax.ppermute(block, axis, route)


def route_tables(expert_ids, gate_weights, flight):
    experts = jnp.arange(flight, dtype=jnp.int32)
    match = (expert_ids[:, :, None] == experts).astype(jnp.float32)
    hits = jnp.sum(match, axis=1)
    chosen = jnp.sum(match * gate_weights[:, :, None], axis=1)
    slots = jnp.cumsum(hits, axis=0) - 1.0
    levels = jnp.arange(CAP, dtype=jnp.float32)
    place = hits.T[:, None, :] * (slots.T[:, None, :] == levels[None, :, None]).astype(jnp.float32)
    return (place, chosen)


def expert_rows(slot_rows, scaled, gate_cols, up_cols, down_rows):
    gate_pre = jnp.dot(slot_rows, gate_cols, preferred_element_type=jnp.float32)
    up_pre = jnp.dot(slot_rows, up_cols, preferred_element_type=jnp.float32)
    sigma = jax.nn.sigmoid(gate_pre)
    active = gate_pre * sigma
    hidden = (active * up_pre).astype(jnp.bfloat16)
    out_part = jnp.dot(hidden, down_rows, preferred_element_type=jnp.float32).astype(jnp.bfloat16)
    dhidden = jnp.dot(scaled, down_rows.T, preferred_element_type=jnp.float32)
    dgate = (dhidden * up_pre * sigma * (1.0 + gate_pre * (1.0 - sigma))).astype(jnp.bfloat16)
    dup = (dhidden * active).astype(jnp.bfloat16)
    dx_part = jnp.dot(dgate, gate_cols.T, preferred_element_type=jnp.float32)
    dx_part = (dx_part + jnp.dot(dup, up_cols.T, preferred_element_type=jnp.float32)).astype(
        jnp.bfloat16
    )
    grad_g = jnp.dot(slot_rows.T, dgate, preferred_element_type=jnp.float32)
    grad_u = jnp.dot(slot_rows.T, dup, preferred_element_type=jnp.float32)
    grad_d = jnp.dot(hidden.T, scaled, preferred_element_type=jnp.float32)
    return (out_part, dx_part, grad_g, grad_u, grad_d)


def per_device(tokens, cotangent, expert_ids, gate_weights, w_gate, w_up, w_down):
    pipe_count = lax.axis_size("pipe")
    pipe_rank = lax.axis_index("pipe")
    owners = lax.axis_size("expert")
    flight = owners // GROUP
    width = tokens.shape[1]
    middle = width // 2
    front_half = pipe_rank < pipe_count // 2
    pipe_bits = pipe_count.bit_length() - 1
    highest = lax.Precision.HIGHEST
    own_parts = (w_gate[0], w_up[0], w_down[0])
    mirrored = own_parts
    for level in range(pipe_bits):
        mirrored = swapped((mirrored[0], mirrored[1], mirrored[2]), "pipe", level)
    gate_cols = jnp.concatenate(
        [
            jnp.where(front_half, own_parts[0], mirrored[0]),
            jnp.where(front_half, mirrored[0], own_parts[0]),
        ],
        axis=0,
    )
    up_cols = jnp.concatenate(
        [
            jnp.where(front_half, own_parts[1], mirrored[1]),
            jnp.where(front_half, mirrored[1], own_parts[1]),
        ],
        axis=0,
    )
    down_rows = jnp.concatenate(
        [
            jnp.where(front_half, own_parts[2], mirrored[2]),
            jnp.where(front_half, mirrored[2], own_parts[2]),
        ],
        axis=1,
    )
    place, chosen = route_tables(expert_ids, gate_weights, flight)
    tok_count = tokens.shape[0]
    place_flat = place.reshape(flight * CAP, tok_count).astype(jnp.bfloat16)
    send_rows = jnp.dot(place_flat, tokens, preferred_element_type=jnp.float32).astype(jnp.bfloat16)
    gate_slot = jnp.einsum("ect,te->ec", place, chosen, precision=highest)
    raw_cot = jnp.dot(place_flat, cotangent, preferred_element_type=jnp.float32)
    send_scaled = (gate_slot.reshape(-1, 1) * raw_cot).astype(jnp.bfloat16)
    copies_rows = jnp.repeat(send_rows.reshape(flight, CAP, width), GROUP, axis=0)
    copies_scaled = jnp.repeat(send_scaled.reshape(flight, CAP, width), GROUP, axis=0)
    arrived = (
        lax.all_to_all(copies_rows, "expert", split_axis=0, concat_axis=0, tiled=True),
        lax.all_to_all(copies_scaled, "expert", split_axis=0, concat_axis=0, tiled=True),
    )
    result = expert_rows(
        arrived[0].reshape(-1, width), arrived[1].reshape(-1, width), gate_cols, up_cols, down_rows
    )
    out_part, dx_part, grad_g, grad_u, grad_d = result
    returned = (
        lax.all_to_all(
            out_part.reshape(owners, CAP, width), "expert", split_axis=0, concat_axis=0, tiled=True
        ),
        lax.all_to_all(
            dx_part.reshape(owners, CAP, width), "expert", split_axis=0, concat_axis=0, tiled=True
        ),
    )
    out_sum = jnp.sum(returned[0].astype(jnp.float32).reshape(flight, GROUP, CAP, width), axis=1)
    dx_sum = jnp.sum(returned[1].astype(jnp.float32).reshape(flight, GROUP, CAP, width), axis=1)
    mixed_out = jnp.einsum(
        "ect,ecd->td", place, gate_slot[..., None] * out_sum, precision=highest
    ).astype(jnp.bfloat16)
    input_grad = jnp.einsum("ect,ecd->td", place, dx_sum, precision=highest).astype(jnp.bfloat16)
    lower_g, upper_g = (grad_g[:middle], grad_g[middle:])
    lower_u, upper_u = (grad_u[:middle], grad_u[middle:])
    lower_d, upper_d = (grad_d[:, :middle], grad_d[:, middle:])
    mine_g = jnp.where(front_half, lower_g, upper_g)
    mine_u = jnp.where(front_half, lower_u, upper_u)
    mine_d = jnp.where(front_half, lower_d, upper_d)
    travel = (
        jnp.where(front_half, upper_g, lower_g).astype(jnp.bfloat16),
        jnp.where(front_half, upper_u, lower_u).astype(jnp.bfloat16),
        jnp.where(front_half, upper_d, lower_d).astype(jnp.bfloat16),
    )
    for level in range(pipe_bits):
        travel = swapped((travel[0], travel[1], travel[2]), "pipe", level)
    travel = tuple((part.astype(jnp.float32) for part in travel))
    own_round = lax.optimization_barrier(
        (mine_g.astype(jnp.bfloat16), mine_u.astype(jnp.bfloat16), mine_d.astype(jnp.bfloat16))
    )
    grad_gate = (own_round[0].astype(jnp.float32) + travel[0]).astype(jnp.bfloat16)[None]
    grad_up = (own_round[1].astype(jnp.float32) + travel[1]).astype(jnp.bfloat16)[None]
    grad_down = (own_round[2].astype(jnp.float32) + travel[2]).astype(jnp.bfloat16)[None]
    return (mixed_out, input_grad, grad_gate, grad_up, grad_down)


def solution(mesh):
    return jax.shard_map(
        per_device,
        mesh=mesh,
        in_specs=(
            P(("pipe", "expert"), None),
            P(("pipe", "expert"), None),
            P(("pipe", "expert"), None),
            P(("pipe", "expert"), None),
            P("pipe", None, "expert"),
            P("pipe", None, "expert"),
            P("pipe", "expert", None),
        ),
        out_specs=(
            P(("pipe", "expert"), None),
            P(("pipe", "expert"), None),
            P("pipe", None, "expert"),
            P("pipe", None, "expert"),
            P("pipe", "expert", None),
        ),
        check_vma=False,
    )
```

profile of v0, /device:TPU:33, one launch (start us, length us, event | category | flops | bytes accessed | tf_op | source)
XLA Modules:
  0.0 707.8 jit_solution(13921443990849547220)
XLA Ops:
  4.8 13.0 %all-to-all-start = ((bf16[32,8,7168]{2,1,0:T(8,128)(2,1)}), bf16[32,8,7168]{2,1,0:T(8,128)(2,1)}, u32[]{:S(2)}, u32[]{:S(2)}) async-start(bf16[32,8,7168]{2,1,0:T(8,128)(2,1)} %bitcast.86), calls=%async_computation | async-start | bytes 7340032 | tf_op jit(solution)/shard_map/all_to_all | solution.py:96
  18.5 86.0 %all-to-all-done = bf16[32,8,7168]{2,1,0:T(8,128)(2,1)} async-done(((bf16[32,8,7168]{2,1,0:T(8,128)(2,1)}), bf16[32,8,7168]{2,1,0:T(8,128)(2,1)}, u32[]{:S(2)}, u32[]{:S(2)}) %all-to-all-start) | async-done | bytes 3670048 | tf_op jit(solution)/shard_map/all_to_all | solution.py:96
  106.9 5.7 all-to-all-start.2
  120.6 80.7 %collective-permute-done.7 = bf16[128,3584]{1,0:T(8,128)(2,1)} collective-permute-done((bf16[128,3584]{1,0:T(8,128)(2,1)S(1)}, bf16[128,3584]{1,0:T(8,128)(2,1)}, u32[]{:S(2)}, u32[]{:S(2)}) %collective-permute-start.7) | collective-permute-done | bytes 917536 | tf_op jit(solution)/shard_map/ppermute | solution.py:17
  201.4 39.4 %collective-permute-done.4 = bf16[3584,128]{1,0:T(8,128)(2,1)} collective-permute-done((bf16[3584,128]{1,0:T(8,128)(2,1)}, bf16[3584,128]{1,0:T(8,128)(2,1)}, u32[]{:S(2)}, u32[]{:S(2)}) %collective-permute-start.4) | collective-permute-done | bytes 917536 | tf_op jit(solution)/shard_map/ppermute | solution.py:17
  240.8 19.8 %collective-permute-done.1 = bf16[3584,128]{1,0:T(8,128)(2,1)} collective-permute-done((bf16[3584,128]{1,0:T(8,128)(2,1)}, bf16[3584,128]{1,0:T(8,128)(2,1)}, u32[]{:S(2)}, u32[]{:S(2)}) %collective-permute-start.1) | collective-permute-done | bytes 917536 | tf_op jit(solution)/shard_map/ppermute | solution.py:17
  261.9 50.7 %collective-permute-done.5 = bf16[3584,128]{1,0:T(8,128)(2,1)S(1)} collective-permute-done((bf16[3584,128]{1,0:T(8,128)(2,1)}, bf16[3584,128]{1,0:T(8,128)(2,1)S(1)}, u32[]{:S(2)}, u32[]{:S(2)}) %collective-permute-start.5) | collective-permute-done | bytes 917536 | tf_op jit(solution)/shard_map/ppermute | solution.py:17
  312.8 19.5 %collective-permute-done.2 = bf16[3584,128]{1,0:T(8,128)(2,1)S(1)} collective-permute-done((bf16[3584,128]{1,0:T(8,128)(2,1)}, bf16[3584,128]{1,0:T(8,128)(2,1)S(1)}, u32[]{:S(2)}, u32[]{:S(2)}) %collective-permute-start.2) | collective-permute-done | bytes 917536 | tf_op jit(solution)/shard_map/ppermute | solution.py:17
  333.4 3.5 fusion.16
  336.9 3.8 fusion.10
  340.7 3.3 multiply_convert_fusion.1
  344.1 3.0 fusion.2
  347.0 8.3 %all-to-all-start.1 = ((bf16[32,8,7168]{2,1,0:T(8,128)(2,1)}), bf16[32,8,7168]{2,1,0:T(8,128)(2,1)}, u32[]{:S(2)}, u32[]{:S(2)}) async-start(bf16[32,8,7168]{2,1,0:T(8,128)(2,1)} %fusion.2), calls=%async_computation.1 | async-start | bytes 7340032 | tf_op jit(solution)/shard_map/all_to_all | solution.py:104
  355.3 2.7 fusion.8
  359.4 4.8 collective-permute-start.15
  364.2 3.2 fusion.14
  367.4 4.5 fusion.12
  373.4 2.9 fusion.1
  376.3 45.2 %all-to-all-done.1 = bf16[32,8,7168]{2,1,0:T(8,128)(2,1)} async-done(((bf16[32,8,7168]{2,1,0:T(8,128)(2,1)}), bf16[32,8,7168]{2,1,0:T(8,128)(2,1)}, u32[]{:S(2)}, u32[]{:S(2)}) %all-to-all-start.1) | async-done | bytes 3670048 | tf_op jit(solution)/shard_map/all_to_all | solution.py:104
  421.5 7.2 %all-to-all-start.3 = ((bf16[32,8,7168]{2,1,0:T(8,128)(2,1)}), bf16[32,8,7168]{2,1,0:T(8,128)(2,1)}, u32[]{:S(2)}, u32[]{:S(2)}) async-start(bf16[32,8,7168]{2,1,0:T(8,128)(2,1)} %fusion.1), calls=%async_computation.3 | async-start | bytes 7340032 | tf_op jit(solution)/shard_map/all_to_all | solution.py:107
  430.6 6.1 collective-permute-start.12
  436.8 74.0 %collective-permute-start.16 = (bf16[128,3584]{1,0:T(8,128)(2,1)}, bf16[128,3584]{1,0:T(8,128)(2,1)S(1)}, u32[]{:S(2)}, u32[]{:S(2)}) collective-permute-start(bf16[128,3584]{1,0:T(8,128)(2,1)} %collective-permute-done.15), channel_id=1, source_target_pairs={{0,64},{64,0},{32,96},{96,32},{128,192},{192,128},{160,224},{224,1... | collective-permute-start | bytes 2752520 | tf_op jit(solution)/shard_map/ppermute | solution.py:17
  514.1 49.5 %collective-permute-done.16 = bf16[128,3584]{1,0:T(8,128)(2,1)S(1)} collective-permute-done((bf16[128,3584]{1,0:T(8,128)(2,1)}, bf16[128,3584]{1,0:T(8,128)(2,1)S(1)}, u32[]{:S(2)}, u32[]{:S(2)}) %collective-permute-start.16) | collective-permute-done | bytes 917536 | tf_op jit(solution)/shard_map/ppermute | solution.py:17
  563.6 19.7 %collective-permute-done.13 = bf16[3584,128]{1,0:T(8,128)(2,1)S(1)} collective-permute-done((bf16[3584,128]{1,0:T(8,128)(2,1)S(1)}, bf16[3584,128]{1,0:T(8,128)(2,1)S(1)}, u32[]{:S(2)}, u32[]{:S(2)}) %collective-permute-start.13) | collective-permute-done | bytes 917536 | tf_op jit(solution)/shard_map/ppermute | solution.py:17
  583.2 11.7 %collective-permute-start.14 = (bf16[3584,128]{1,0:T(8,128)(2,1)S(1)}, bf16[3584,128]{1,0:T(8,128)(2,1)S(1)}, u32[]{:S(2)}, u32[]{:S(2)}) collective-permute-start(bf16[3584,128]{1,0:T(8,128)(2,1)S(1)} %collective-permute-done.13), channel_id=1, source_target_pairs={{0,128},{128,0},{32,160},{160,32},{64,192},{192,64},{96,224},{224,... | collective-permute-start | bytes 2752520 | tf_op jit(solution)/shard_map/ppermute | solution.py:17
  594.9 8.0 %collective-permute-done.10 = bf16[3584,128]{1,0:T(8,128)(2,1)S(1)} collective-permute-done((bf16[3584,128]{1,0:T(8,128)(2,1)S(1)}, bf16[3584,128]{1,0:T(8,128)(2,1)S(1)}, u32[]{:S(2)}, u32[]{:S(2)}) %collective-permute-start.10) | collective-permute-done | bytes 917536 | tf_op jit(solution)/shard_map/ppermute | solution.py:17
  602.9 21.3 %collective-permute-start.11 = (bf16[3584,128]{1,0:T(8,128)(2,1)S(1)}, bf16[3584,128]{1,0:T(8,128)(2,1)S(1)}, u32[]{:S(2)}, u32[]{:S(2)}) collective-permute-start(bf16[3584,128]{1,0:T(8,128)(2,1)S(1)} %collective-permute-done.10), channel_id=1, source_target_pairs={{0,128},{128,0},{32,160},{160,32},{64,192},{192,64},{96,224},{224,... | collective-permute-start | bytes 2752520 | tf_op jit(solution)/shard_map/ppermute | solution.py:17
  625.3 47.8 %collective-permute-done.14 = bf16[3584,128]{1,0:T(8,128)(2,1)S(1)} collective-permute-done((bf16[3584,128]{1,0:T(8,128)(2,1)S(1)}, bf16[3584,128]{1,0:T(8,128)(2,1)S(1)}, u32[]{:S(2)}, u32[]{:S(2)}) %collective-permute-start.14) | collective-permute-done | bytes 917536 | tf_op jit(solution)/shard_map/ppermute | solution.py:17
  674.3 18.5 %collective-permute-done.11 = bf16[3584,128]{1,0:T(8,128)(2,1)S(1)} collective-permute-done((bf16[3584,128]{1,0:T(8,128)(2,1)S(1)}, bf16[3584,128]{1,0:T(8,128)(2,1)S(1)}, u32[]{:S(2)}, u32[]{:S(2)}) %collective-permute-start.11) | collective-permute-done | bytes 917536 | tf_op jit(solution)/shard_map/ppermute | solution.py:17
  696.6 4.3 fusion.3
  700.9 2.7 convert_reduce_fusion
  703.6 4.2 fusion.4
  (79 shorter events, 32.0 us)
Async XLA Ops:
  4.8 13.3 %copy-start.11 = (bf16[128,7168]{1,0:T(8,128)(2,1)S(1)}, bf16[128,7168]{1,0:T(8,128)(2,1)}, u32[]{:S(2)}) copy-start(bf16[128,7168]{1,0:T(8,128)(2,1)} %param.8) | copy-start | bytes 5505028
  4.8 99.7 %all-to-all-start = ((bf16[32,8,7168]{2,1,0:T(8,128)(2,1)}), bf16[32,8,7168]{2,1,0:T(8,128)(2,1)}, u32[]{:S(2)}, u32[]{:S(2)}) async-start(bf16[32,8,7168]{2,1,0:T(8,128)(2,1)} %bitcast.86), calls=%async_computation | async-start | bytes 7340032 | tf_op jit(solution)/shard_map/all_to_all | solution.py:96
  106.9 5.7 copy-start.12
  106.9 8.0 %copy-start.13 = (bf16[1,3584,128]{2,1,0:T(8,128)(2,1)S(1)}, bf16[1,3584,128]{2,1,0:T(8,128)(2,1)}, u32[]{:S(2)}) copy-start(bf16[1,3584,128]{2,1,0:T(8,128)(2,1)} %param.12) | copy-start | bytes 2752516
  106.9 8.1 %copy-start.14 = (bf16[1,3584,128]{2,1,0:T(8,128)(2,1)S(1)}, bf16[1,3584,128]{2,1,0:T(8,128)(2,1)}, u32[]{:S(2)}) copy-start(bf16[1,3584,128]{2,1,0:T(8,128)(2,1)} %param.11) | copy-start | bytes 2752516
  106.9 230.0 %all-to-all-start.2 = ((bf16[32,8,7168]{2,1,0:T(8,128)(2,1)}), bf16[32,8,7168]{2,1,0:T(8,128)(2,1)}, u32[]{:S(2)}, u32[]{:S(2)}) async-start(bf16[32,8,7168]{2,1,0:T(8,128)(2,1)} %bitcast.85), calls=%async_computation.2 | async-start | bytes 7340032 | tf_op jit(solution)/shard_map/all_to_all | solution.py:97
  112.6 4.6 collective-permute-start.6
  114.9 3.5 collective-permute-start.3
  115.0 4.7 collective-permute-start
  117.2 84.2 %collective-permute-start.7 = (bf16[128,3584]{1,0:T(8,128)(2,1)S(1)}, bf16[128,3584]{1,0:T(8,128)(2,1)}, u32[]{:S(2)}, u32[]{:S(2)}) collective-permute-start(bf16[128,3584]{1,0:T(8,128)(2,1)S(1)} %collective-permute-done.6), channel_id=1, source_target_pairs={{0,64},{64,0},{32,96},{96,32},{128,192},{192,128},{160,224},{224,1... | collective-permute-start | bytes 2752520 | tf_op jit(solution)/shard_map/ppermute | solution.py:17
  118.4 122.4 %collective-permute-start.4 = (bf16[3584,128]{1,0:T(8,128)(2,1)}, bf16[3584,128]{1,0:T(8,128)(2,1)}, u32[]{:S(2)}, u32[]{:S(2)}) collective-permute-start(bf16[3584,128]{1,0:T(8,128)(2,1)} %collective-permute-done.3), channel_id=1, source_target_pairs={{0,64},{64,0},{32,96},{96,32},{128,192},{192,128},{160,224},{224,1... | collective-permute-start | bytes 2752520 | tf_op jit(solution)/shard_map/ppermute | solution.py:17
  119.7 140.8 %collective-permute-start.1 = (bf16[3584,128]{1,0:T(8,128)(2,1)}, bf16[3584,128]{1,0:T(8,128)(2,1)}, u32[]{:S(2)}, u32[]{:S(2)}) collective-permute-start(bf16[3584,128]{1,0:T(8,128)(2,1)} %collective-permute-done), channel_id=1, source_target_pairs={{0,64},{64,0},{32,96},{96,32},{128,192},{192,128},{160,224},{224,1... | collective-permute-start | bytes 2752520 | tf_op jit(solution)/shard_map/ppermute | solution.py:17
  201.4 59.2 %collective-permute-start.8 = (bf16[128,3584]{1,0:T(8,128)(2,1)}, bf16[128,3584]{1,0:T(8,128)(2,1)S(1)}, u32[]{:S(2)}, u32[]{:S(2)}) collective-permute-start(bf16[128,3584]{1,0:T(8,128)(2,1)} %collective-permute-done.7), channel_id=1, source_target_pairs={{0,128},{128,0},{32,160},{160,32},{64,192},{192,64},{96,224},{224,... | collective-permute-start | bytes 2752520 | tf_op jit(solution)/shard_map/ppermute | solution.py:17
  201.4 130.9 %copy-start.15 = (bf16[1,3584,128]{2,1,0:T(8,128)(2,1)S(1)}, bf16[1,3584,128]{2,1,0:T(8,128)(2,1)}, u32[]{:S(2)}) copy-start(bf16[1,3584,128]{2,1,0:T(8,128)(2,1)} %param.11) | copy-start | bytes 2752516
  240.8 71.8 %collective-permute-start.5 = (bf16[3584,128]{1,0:T(8,128)(2,1)}, bf16[3584,128]{1,0:T(8,128)(2,1)S(1)}, u32[]{:S(2)}, u32[]{:S(2)}) collective-permute-start(bf16[3584,128]{1,0:T(8,128)(2,1)} %collective-permute-done.4), channel_id=1, source_target_pairs={{0,128},{128,0},{32,160},{160,32},{64,192},{192,64},{96,224},{224,... | collective-permute-start | bytes 2752520 | tf_op jit(solution)/shard_map/ppermute | solution.py:17
  260.6 71.7 %collective-permute-start.2 = (bf16[3584,128]{1,0:T(8,128)(2,1)}, bf16[3584,128]{1,0:T(8,128)(2,1)S(1)}, u32[]{:S(2)}, u32[]{:S(2)}) collective-permute-start(bf16[3584,128]{1,0:T(8,128)(2,1)} %collective-permute-done.1), channel_id=1, source_target_pairs={{0,128},{128,0},{32,160},{160,32},{64,192},{192,64},{96,224},{224,... | collective-permute-start | bytes 2752520 | tf_op jit(solution)/shard_map/ppermute | solution.py:17
  312.8 24.1 %copy-start.2 = (bf16[3584,128]{1,0:T(8,128)(2,1)}, bf16[3584,128]{1,0:T(8,128)(2,1)S(1)}, u32[]{:S(2)}) copy-start(bf16[3584,128]{1,0:T(8,128)(2,1)S(1)} %get-tuple-element.24) | copy-start | bytes 2752516
  333.3 7.3 %copy-start.4 = (bf16[3584,128]{1,0:T(8,128)(2,1)}, bf16[3584,128]{1,0:T(8,128)(2,1)S(1)}, u32[]{:S(2)}) copy-start(bf16[3584,128]{1,0:T(8,128)(2,1)S(1)} %get-tuple-element.21) | copy-start | bytes 2752516
  347.0 74.5 %all-to-all-start.1 = ((bf16[32,8,7168]{2,1,0:T(8,128)(2,1)}), bf16[32,8,7168]{2,1,0:T(8,128)(2,1)}, u32[]{:S(2)}, u32[]{:S(2)}) async-start(bf16[32,8,7168]{2,1,0:T(8,128)(2,1)} %fusion.2), calls=%async_computation.1 | async-start | bytes 7340032 | tf_op jit(solution)/shard_map/all_to_all | solution.py:104
  359.4 77.4 %collective-permute-start.15 = (bf16[128,3584]{1,0:T(8,128)(2,1)}, bf16[128,3584]{1,0:T(8,128)(2,1)}, u32[]{:S(2)}, u32[]{:S(2)}) collective-permute-start(bf16[128,3584]{1,0:T(8,128)(2,1)} %get-tuple-element.13), channel_id=1, source_target_pairs={{0,32},{32,0},{64,96},{96,64},{128,160},{160,128},{192,224},{224,1... | collective-permute-start | bytes 2752520 | tf_op jit(solution)/shard_map/ppermute | solution.py:17
  367.4 4.5 copy-start.3
  421.5 279.4 %all-to-all-start.3 = ((bf16[32,8,7168]{2,1,0:T(8,128)(2,1)}), bf16[32,8,7168]{2,1,0:T(8,128)(2,1)}, u32[]{:S(2)}, u32[]{:S(2)}) async-start(bf16[32,8,7168]{2,1,0:T(8,128)(2,1)} %fusion.1), calls=%async_computation.3 | async-start | bytes 7340032 | tf_op jit(solution)/shard_map/all_to_all | solution.py:107
  428.8 195.4 %copy-start.8 = (bf16[128,3584]{1,0:T(8,128)(2,1)S(1)}, bf16[128,3584]{1,0:T(8,128)(2,1)}, u32[]{:S(2)}) copy-start(bf16[128,3584]{1,0:T(8,128)(2,1)} %get-tuple-element.10) | copy-start | bytes 2752516
  430.6 80.2 %collective-permute-start.12 = (bf16[3584,128]{1,0:T(8,128)(2,1)S(1)}, bf16[3584,128]{1,0:T(8,128)(2,1)S(1)}, u32[]{:S(2)}, u32[]{:S(2)}) collective-permute-start(bf16[3584,128]{1,0:T(8,128)(2,1)S(1)} %get-tuple-element.15), channel_id=1, source_target_pairs={{0,32},{32,0},{64,96},{96,64},{128,160},{160,128},{192,224},{224,1... | collective-permute-start | bytes 2752520 | tf_op jit(solution)/shard_map/ppermute | solution.py:17
  436.7 76.1 %collective-permute-start.9 = (bf16[3584,128]{1,0:T(8,128)(2,1)S(1)}, bf16[3584,128]{1,0:T(8,128)(2,1)S(1)}, u32[]{:S(2)}, u32[]{:S(2)}) collective-permute-start(bf16[3584,128]{1,0:T(8,128)(2,1)S(1)} %get-tuple-element.18), channel_id=1, source_target_pairs={{0,32},{32,0},{64,96},{96,64},{128,160},{160,128},{192,224},{224,1... | collective-permute-start | bytes 2752520 | tf_op jit(solution)/shard_map/ppermute | solution.py:17
  436.8 126.8 %collective-permute-start.16 = (bf16[128,3584]{1,0:T(8,128)(2,1)}, bf16[128,3584]{1,0:T(8,128)(2,1)S(1)}, u32[]{:S(2)}, u32[]{:S(2)}) collective-permute-start(bf16[128,3584]{1,0:T(8,128)(2,1)} %collective-permute-done.15), channel_id=1, source_target_pairs={{0,64},{64,0},{32,96},{96,32},{128,192},{192,128},{160,224},{224,1... | collective-permute-start | bytes 2752520 | tf_op jit(solution)/shard_map/ppermute | solution.py:17
  510.8 72.5 %collective-permute-start.13 = (bf16[3584,128]{1,0:T(8,128)(2,1)S(1)}, bf16[3584,128]{1,0:T(8,128)(2,1)S(1)}, u32[]{:S(2)}, u32[]{:S(2)}) collective-permute-start(bf16[3584,128]{1,0:T(8,128)(2,1)S(1)} %collective-permute-done.12), channel_id=1, source_target_pairs={{0,64},{64,0},{32,96},{96,32},{128,192},{192,128},{160,224},{224,1... | collective-permute-start | bytes 2752520 | tf_op jit(solution)/shard_map/ppermute | solution.py:17
  512.8 90.1 %collective-permute-start.10 = (bf16[3584,128]{1,0:T(8,128)(2,1)S(1)}, bf16[3584,128]{1,0:T(8,128)(2,1)S(1)}, u32[]{:S(2)}, u32[]{:S(2)}) collective-permute-start(bf16[3584,128]{1,0:T(8,128)(2,1)S(1)} %collective-permute-done.9), channel_id=1, source_target_pairs={{0,64},{64,0},{32,96},{96,32},{128,192},{192,128},{160,224},{224,1... | collective-permute-start | bytes 2752520 | tf_op jit(solution)/shard_map/ppermute | solution.py:17
  563.6 60.6 %collective-permute-start.17 = (bf16[128,3584]{1,0:T(8,128)(2,1)S(1)}, bf16[128,3584]{1,0:T(8,128)(2,1)S(1)}, u32[]{:S(2)}, u32[]{:S(2)}) collective-permute-start(bf16[128,3584]{1,0:T(8,128)(2,1)S(1)} %collective-permute-done.16), channel_id=1, source_target_pairs={{0,128},{128,0},{32,160},{160,32},{64,192},{192,64},{96,224},{224,... | collective-permute-start | bytes 2752520 | tf_op jit(solution)/shard_map/ppermute | solution.py:17
  583.2 89.9 %collective-permute-start.14 = (bf16[3584,128]{1,0:T(8,128)(2,1)S(1)}, bf16[3584,128]{1,0:T(8,128)(2,1)S(1)}, u32[]{:S(2)}, u32[]{:S(2)}) collective-permute-start(bf16[3584,128]{1,0:T(8,128)(2,1)S(1)} %collective-permute-done.13), channel_id=1, source_target_pairs={{0,128},{128,0},{32,160},{160,32},{64,192},{192,64},{96,224},{224,... | collective-permute-start | bytes 2752520 | tf_op jit(solution)/shard_map/ppermute | solution.py:17
  602.9 89.9 %collective-permute-start.11 = (bf16[3584,128]{1,0:T(8,128)(2,1)S(1)}, bf16[3584,128]{1,0:T(8,128)(2,1)S(1)}, u32[]{:S(2)}, u32[]{:S(2)}) collective-permute-start(bf16[3584,128]{1,0:T(8,128)(2,1)S(1)} %collective-permute-done.10), channel_id=1, source_target_pairs={{0,128},{128,0},{32,160},{160,32},{64,192},{192,64},{96,224},{224,... | collective-permute-start | bytes 2752520 | tf_op jit(solution)/shard_map/ppermute | solution.py:17
  696.6 11.2 %copy-start.1 = (bf16[128,7168]{1,0:T(8,128)(2,1)S(1)}, bf16[128,7168]{1,0:T(8,128)(2,1)}, u32[]{:S(2)}) copy-start(bf16[128,7168]{1,0:T(8,128)(2,1)} %param.7) | copy-start | bytes 5505028
  (6 other events, 14.6 us)
where the time goes:
time: 712 us; the launch traced here: 708 us
  waiting for transfers between devices  487 us (68%)
  starting transfers between devices  161 us (23%)
  matrix products  37.6 us (5%)
  other arithmetic  15.5 us (2%)
    ppermute x18, waiting for transfers between devices, swapped(): return lax.ppermute(block, axis, route)  356 us
    ppermute x18, starting transfers between devices, swapped(): return lax.ppermute(block, axis, route)  127 us
    all_to_all x1, waiting for transfers between devices, per_device(): lax.all_to_all(copies_rows, 'expert', split_axis=0, concat_axis=0, tiled=...  86 us
    all_to_all x1, waiting for transfers between devices, per_device(): lax.all_to_all(out_part.reshape(owners, CAP, width), 'expert', split_axis...  45.2 us
  transfers between devices with their start and end apart: 22, of which 15 were waited for; matrix products, arithmetic and copies ran while one was open for 5% of the time, Pallas kernels for 0%

commit v1 on v0

v1 whole, which is shorter than its diff:
```python
import functools

import jax
import jax.numpy as jnp
from jax import lax
from jax.experimental import pallas as pl
from jax.experimental.pallas import tpu as pltpu
from jax.sharding import PartitionSpec as P

GROUP = 8
CAP = 8
NY = 4
NX = 4
STAGES = 4
TILE = 512
MESH = pl.DeviceIdType.MESH
F32 = jnp.float32
BF16 = jnp.bfloat16


def route_tables(expert_ids, gate_weights, flight):
    experts = jnp.arange(flight, dtype=jnp.int32)
    match = (expert_ids[:, :, None] == experts).astype(F32)
    hits = jnp.sum(match, axis=1)
    chosen = jnp.sum(match * gate_weights[:, :, None], axis=1)
    slots = jnp.cumsum(hits, axis=0) - 1.0
    levels = jnp.arange(CAP, dtype=F32)
    place = hits.T[:, None, :] * (slots.T[:, None, :] == levels[None, :, None]).astype(F32)
    return place, chosen


def dot(a, b):
    return jnp.dot(a, b, preferred_element_type=F32)


def loop(n, body):
    def step(i, carry):
        body(i)
        return carry

    lax.fori_loop(0, n, step, 0)


def kernel(
    tok_hbm, cot_hbm, place_hbm, gsl_hbm, wg_hbm, wu_hbm, wd_hbm,
    mixed_hbm, igrad_hbm, gg_hbm, gu_hbm, gd_hbm,
    tok, cot, place, gsl, wgu, wguT, wd, wdT, sb, xs, x2d, s2d, part, pbs, pbr,
    h16, dgu16, ob, mid, rb, fb, mixed, igrad, gg, gu, gd,
    in_sem, out_sem, zsend, xsend, xfsend, recv, psend, precv, msend, mrecv, rsend, rrecv, osend, orecv,
):
    half = wd.shape[1]
    tiles = half // TILE
    p = lax.axis_index("pipe")
    e = lax.axis_index("expert")
    y = lax.div(e, 8)
    zh = lax.rem(lax.div(e, 4), 2)
    x = lax.rem(e, 4)
    h = lax.div(p, 4)
    q = p + h * (7 - 2 * p)
    right = lax.rem(x + 1, 4)
    left = lax.rem(x + 3, 4)
    across = lax.rem(x + 2, 4)
    yz = e - x

    def rank_of(hh):
        return q + hh * (7 - 2 * q)

    def flip(i):
        return lax.rem(lax.div(i, 2) + lax.div(q, 2), 2) * 2 + lax.rem(lax.rem(i, 2) + lax.rem(q, 2), 2)

    own_s = (h * 2 + zh) * 4 + y
    own_stage = flip(h * 2 + zh)

    def remote(src, dst, ssem, rsem, rank, expert):
        return pltpu.make_async_remote_copy(
            src_ref=src, dst_ref=dst, send_sem=ssem, recv_sem=rsem,
            device_id=(rank, expert), device_id_type=MESH)

    def arrived(ref, sem):
        pltpu.make_async_copy(ref, ref, sem).wait()

    def peer(t):
        j, d = lax.div(t, 4), lax.rem(t, 4)
        hh = lax.rem(h + lax.div(d, 2), 2)
        zz = lax.rem(zh + lax.rem(d, 2), 2)
        yy = lax.rem(y + 4 - j, 4)
        return hh, zz, yy

    barrier = pltpu.get_barrier_semaphore()

    def greet(t):
        hh, zz, yy = peer(t + 1)
        pl.semaphore_signal(barrier, inc=1, device_id=(rank_of(hh), yy * 8 + zz * 4 + x), device_id_type=MESH)

    loop(15, greet)
    pl.semaphore_signal(barrier, inc=1, device_id=(p, yz + right), device_id_type=MESH)
    pl.semaphore_signal(barrier, inc=1, device_id=(p, yz + left), device_id_type=MESH)

    loads = [
        pltpu.make_async_copy(place_hbm, place, in_sem.at[0]),
        pltpu.make_async_copy(gsl_hbm, gsl, in_sem.at[1]),
        pltpu.make_async_copy(tok_hbm, tok, in_sem.at[2]),
        pltpu.make_async_copy(cot_hbm, cot, in_sem.at[3]),
        pltpu.make_async_copy(wg_hbm, wgu.at[:, pl.ds(0, 128)], in_sem.at[4]),
        pltpu.make_async_copy(wu_hbm, wgu.at[:, pl.ds(128, 128)], in_sem.at[5]),
        pltpu.make_async_copy(wd_hbm, wd, in_sem.at[6]),
    ]
    for load in loads:
        load.start()
    for load in loads[:4]:
        load.wait()

    def slot_rows(ct):
        hf, col = lax.div(ct, tiles), lax.rem(ct, tiles) * TILE
        cols = pl.ds(pl.multiple_of(ct * TILE, TILE), TILE)
        to = pl.ds(pl.multiple_of(col, TILE), TILE)
        rows = dot(place[...], tok[:, cols])
        sb[:, hf, 0, :, to] = rows.reshape(NY, CAP, TILE).astype(BF16)
        raw = dot(place[...], cot[:, cols]) * gsl[...]
        sb[:, hf, 1, :, to] = raw.reshape(NY, CAP, TILE).astype(BF16)

    loop(2 * tiles, slot_rows)
    pl.semaphore_wait(barrier, 17)

    local = pltpu.make_async_copy(sb.at[y, h], xs.at[x, own_s], recv.at[x, own_s])

    def zcopy(t):
        hh, zz, yy = peer(t)
        return remote(sb.at[yy, hh], xs.at[x, own_s], zsend.at[t], recv.at[x, own_s],
                      rank_of(hh), yy * 8 + zz * 4 + x)

    def send_out(stage):
        @pl.when(own_stage == stage)
        def _():
            local.start()
            loop(15, lambda t: zcopy(t + 1).start())

    def source(i, j):
        return flip(i) * 4 + lax.rem(y + j, 4)

    def xcopy(s, side):
        return remote(xs.at[x, s], xs.at[x, s], xsend.at[side, s], recv.at[x, s],
                      p, yz + (right if side == 0 else left))

    def xforward(s):
        odd = lax.rem(s, 2)
        c = lax.rem(x + 3 + 2 * odd, 4)
        to = lax.rem(x + 1 + 2 * odd, 4)
        return remote(xs.at[c, s], xs.at[c, s], xfsend.at[s], recv.at[c, s], p, yz + to)

    def gather_own(i):
        def one(j):
            s = source(i, j)
            arrived(xs.at[x, s], recv.at[x, s])
            xcopy(s, 0).start()
            xcopy(s, 1).start()

        loop(4, one)

    def gather_forward(i):
        def one(j):
            s = source(i, j)
            c = lax.rem(x + 3 + 2 * lax.rem(s, 2), 4)
            arrived(xs.at[c, s], recv.at[c, s])
            xforward(s).start()

        loop(4, one)

    def gather_rest(i):
        def one(j):
            s = source(i, j)
            c = lax.rem(x + 1 + 2 * lax.rem(s, 2), 4)
            arrived(xs.at[c, s], recv.at[c, s])
            arrived(xs.at[across, s], recv.at[across, s])

        loop(4, one)

    def pcopy(i):
        return remote(pbs.at[i], pbr.at[i], psend.at[i], precv.at[i], 7 - p, e)

    def rows_of(i):
        return pl.ds(pl.multiple_of(i * 128, 128), 128)

    def first_dots(i):
        g4 = flip(i) * 4

        def flatten(c):
            to = pl.ds(pl.multiple_of(i * 128 + c * 32, 32), 32)
            x2d[to, :] = xs[c, pl.ds(g4, 4), 0].astype(F32).reshape(32, half).astype(BF16)
            s2d[to, :] = xs[c, pl.ds(g4, 4), 1].astype(F32).reshape(32, half).astype(BF16)

        loop(4, flatten)
        rows = rows_of(i)
        part[i, :, 0:256] = dot(x2d[rows, :], wgu[...])
        part[i, :, 256:384] = dot(s2d[rows, :], wdT[...])
        pbs[i] = part[i].reshape(16, 8, 384).astype(BF16)
        pcopy(i).start()

    def mid_copy(s):
        to = lax.rem(x + 3 + 2 * lax.rem(s, 2), 4)
        return remote(ob.at[across, s], mid.at[s], msend.at[s], mrecv.at[s], p, yz + to)

    def near_copy(s, side):
        c = left if side == 0 else right
        return remote(ob.at[c, s], rb.at[side, s], rsend.at[side, s], rrecv.at[side, s], p, yz + c)

    def near_copy_by(s, side):
        c = lax.rem(x + 3 + 2 * side, 4)
        return remote(ob.at[c, s], rb.at[side, s], rsend.at[side, s], rrecv.at[side, s], p, yz + c)

    def second_dots(i):
        g4 = flip(i) * 4
        rows = rows_of(i)
        arrived(pbr.at[i], precv.at[i])
        whole = part[i] + pbr[i].astype(F32).reshape(128, 384)
        gate, up, dh = whole[:, 0:128], whole[:, 128:256], whole[:, 256:384]
        sigma = jax.nn.sigmoid(gate)
        active = gate * sigma
        h16[rows, :] = (active * up).astype(BF16)
        dgu16[rows, 0:128] = (dh * up * sigma * (1.0 + gate * (1.0 - sigma))).astype(BF16)
        dgu16[rows, 128:256] = (dh * active).astype(BF16)

        def tile(ct):
            cols = pl.ds(pl.multiple_of(ct * TILE, TILE), TILE)
            out = dot(h16[rows, :], wd[:, cols])
            ob[:, pl.ds(g4, 4), 0, :, cols] = out.reshape(NX, NY, CAP, TILE).astype(BF16)
            back = dot(dgu16[rows, :], wguT[:, cols])
            ob[:, pl.ds(g4, 4), 1, :, cols] = back.reshape(NX, NY, CAP, TILE).astype(BF16)

        loop(tiles, tile)
        loop(4, lambda j: mid_copy(source(i, j)).start())

        def direct(j):
            s = source(i, j)
            near_copy_by(s, 1 - lax.rem(s, 2)).start()

        loop(4, direct)

    def add_mid(i):
        def one(j):
            s = source(i, j)
            odd = lax.rem(s, 2)
            c = lax.rem(x + 3 + 2 * odd, 4)
            arrived(mid.at[s], mrecv.at[s])
            ob[c, s] = (ob[c, s].astype(F32) + mid[s].astype(F32)).astype(BF16)
            near_copy_by(s, odd).start()

        loop(4, one)

    def owner_copy(s):
        g = lax.div(s, 4)
        return remote(ob.at[x, s], fb.at[y, h, zh], osend.at[s], orecv.at[(y * 2 + h) * 2 + zh],
                      rank_of(lax.div(g, 2)), lax.rem(s, 4) * 8 + lax.rem(g, 2) * 4 + x)

    own_out = pltpu.make_async_copy(ob.at[x, own_s], fb.at[y, h, zh], orecv.at[(y * 2 + h) * 2 + zh])

    def add_last(i):
        def one(j):
            s = source(i, j)
            arrived(rb.at[0, s], rrecv.at[0, s])
            arrived(rb.at[1, s], rrecv.at[1, s])
            ob[x, s] = (ob[x, s].astype(F32) + rb[0, s].astype(F32) + rb[1, s].astype(F32)).astype(BF16)

            @pl.when(s == own_s)
            def _():
                own_out.start()

            @pl.when(s != own_s)
            def _():
                owner_copy(s).start()

        loop(4, one)

    send_out(0)
    send_out(1)
    for load in loads[4:]:
        load.wait()

    def turn(ct):
        cols = pl.ds(pl.multiple_of(ct * TILE, TILE), TILE)
        wguT[:, cols] = wgu[cols, :].T
        wdT[cols, :] = wd[:, cols].T

    loop(tiles, turn)
    gather_own(0)

    def weight_grads():
        dguT = dgu16[...].T
        hT = h16[...].T

        def tile(ct):
            cols = pl.ds(pl.multiple_of(ct * TILE, TILE), TILE)
            both = dot(dguT, x2d[:, cols]).T
            gg[cols, :] = both[:, 0:128].astype(BF16)
            gu[cols, :] = both[:, 128:256].astype(BF16)
            gd[:, cols] = dot(hT, s2d[:, cols]).astype(BF16)

        loop(tiles, tile)

    def turn_of(i):
        @pl.when(i < 2)
        def _():
            send_out(i + 2)

        @pl.when(i < 4)
        def _():
            gather_forward(i)

        @pl.when(i < 3)
        def _():
            gather_own(i + 1)

        @pl.when(i < 4)
        def _():
            gather_rest(i)
            first_dots(i)

        @pl.when(i >= 2)
        def _():
            add_mid(i - 2)

        @pl.when(jnp.logical_and(i >= 1, i < 5))
        def _():
            second_dots(i - 1)

        @pl.when(i >= 2)
        def _():
            add_last(i - 2)

        @pl.when(i == 4)
        def _():
            weight_grads()

    loop(6, turn_of)

    stores = [
        pltpu.make_async_copy(gg, gg_hbm, out_sem.at[0]),
        pltpu.make_async_copy(gu, gu_hbm, out_sem.at[1]),
        pltpu.make_async_copy(gd, gd_hbm, out_sem.at[2]),
        pltpu.make_async_copy(mixed, mixed_hbm, out_sem.at[3]),
        pltpu.make_async_copy(igrad, igrad_hbm, out_sem.at[4]),
    ]
    for store in stores[:3]:
        store.start()

    def landed(t):
        k, hz = lax.div(t, 4), lax.rem(t, 4)
        hh, zz = lax.div(hz, 2), lax.rem(hz, 2)
        arrived(fb.at[k, hh, zz], orecv.at[t])

    loop(16, landed)

    placeT = place[...].T

    def combine(ct):
        hf, col = lax.div(ct, tiles), lax.rem(ct, tiles) * TILE
        cols = pl.ds(pl.multiple_of(ct * TILE, TILE), TILE)
        fr = pl.ds(pl.multiple_of(col, TILE), TILE)

        def both(k):
            return (fb[:, hf, 0, k, :, fr].astype(F32) + fb[:, hf, 1, k, :, fr].astype(F32)).reshape(32, TILE)

        mixed[:, cols] = dot(placeT, (both(0) * gsl[...]).astype(BF16)).astype(BF16)
        igrad[:, cols] = dot(placeT, both(1).astype(BF16)).astype(BF16)

    loop(2 * tiles, combine)
    for store in stores[3:]:
        store.start()

    loop(15, lambda t: zcopy(t + 1).wait_send())

    def sent(s):
        xcopy(s, 0).wait_send()
        xcopy(s, 1).wait_send()
        xforward(s).wait_send()
        mid_copy(s).wait_send()
        near_copy(s, 0).wait_send()
        near_copy(s, 1).wait_send()

        @pl.when(s != own_s)
        def _():
            owner_copy(s).wait_send()

    loop(16, sent)
    loop(STAGES, lambda i: pcopy(i).wait_send())
    for store in stores:
        store.wait()


def per_device(tokens, cotangent, expert_ids, gate_weights, w_gate, w_up, w_down):
    flight = lax.axis_size("expert") // GROUP
    tok_count, width = tokens.shape
    half = width // 2
    highest = lax.Precision.HIGHEST
    place, chosen = route_tables(expert_ids, gate_weights, flight)
    gate_slot = jnp.einsum("ect,te->ec", place, chosen, precision=highest).reshape(-1, 1)
    place16 = place.reshape(flight * CAP, tok_count).astype(BF16)
    dma = pltpu.SemaphoreType.DMA
    vmem = pltpu.VMEM
    piece = (2, CAP, half)
    any_spec = pl.BlockSpec(memory_space=pl.ANY)
    outs = pl.pallas_call(
        kernel,
        out_shape=(
            jax.ShapeDtypeStruct((tok_count, width), BF16),
            jax.ShapeDtypeStruct((tok_count, width), BF16),
            jax.ShapeDtypeStruct((half, 128), BF16),
            jax.ShapeDtypeStruct((half, 128), BF16),
            jax.ShapeDtypeStruct((128, half), BF16),
        ),
        in_specs=[any_spec] * 7,
        out_specs=[any_spec] * 5,
        scratch_shapes=[
            vmem((tok_count, width), BF16),
            vmem((tok_count, width), BF16),
            vmem((32, tok_count), BF16),
            vmem((32, 1), F32),
            vmem((half, 256), BF16),
            vmem((256, half), BF16),
            vmem((128, half), BF16),
            vmem((half, 128), BF16),
            vmem((NY, 2) + piece, BF16),
            vmem((NX, 16) + piece, BF16),
            vmem((512, half), BF16),
            vmem((512, half), BF16),
            vmem((STAGES, 128, 384), F32),
            vmem((STAGES, 16, 8, 384), BF16),
            vmem((STAGES, 16, 8, 384), BF16),
            vmem((512, 128), BF16),
            vmem((512, 256), BF16),
            vmem((NX, 16) + piece, BF16),
            vmem((16,) + piece, BF16),
            vmem((2, 16) + piece, BF16),
            vmem((NY, 2, 2) + piece, BF16),
            vmem((tok_count, width), BF16),
            vmem((tok_count, width), BF16),
            vmem((half, 128), BF16),
            vmem((half, 128), BF16),
            vmem((128, half), BF16),
            dma((7,)),
            dma((5,)),
            dma((16,)),
            dma((2, 16)),
            dma((16,)),
            dma((NX, 16)),
            dma((STAGES,)),
            dma((STAGES,)),
            dma((16,)),
            dma((16,)),
            dma((2, 16)),
            dma((2, 16)),
            dma((16,)),
            dma((16,)),
        ],
        compiler_params=pltpu.CompilerParams(
            collective_id=0, has_side_effects=True, vmem_limit_bytes=60 * 1024 * 1024
        ),
    )(tokens, cotangent, place16, gate_slot, w_gate[0], w_up[0], w_down[0])
    return outs[0], outs[1], outs[2][None], outs[3][None], outs[4][None]


def solution(mesh):
    return jax.shard_map(
        per_device,
        mesh=mesh,
        in_specs=(
            P(("pipe", "expert"), None),
            P(("pipe", "expert"), None),
            P(("pipe", "expert"), None),
            P(("pipe", "expert"), None),
            P("pipe", None, "expert"),
            P("pipe", None, "expert"),
            P("pipe", "expert", None),
        ),
        out_specs=(
            P(("pipe", "expert"), None),
            P(("pipe", "expert"), None),
            P("pipe", None, "expert"),
            P("pipe", None, "expert"),
            P("pipe", "expert", None),
        ),
        check_vma=False,
    )
```

time: 712 us -> 194 us (0.27)
  waiting for transfers between devices: 487 us -> 0 us
  Pallas kernels: 0 us -> 182 us
  starting transfers between devices: 161 us -> 0 us
  matrix products: 37.6 us -> 0.77 us
  other arithmetic: 15.5 us -> 1.6 us
    ppermute x18 -> x0, waiting for transfers between devices: 356 us -> none  [swapped(): return lax.ppermute(block, axis, route)]
    pallas_call x0 -> x1, Pallas kernels: none -> 182 us  [per_device(): pl.pallas_call(kernel, out_shape=(jax.ShapeDtypeStruct((tok_count, width)...]
    all_to_all x4 -> x0, waiting for transfers between devices: 131 us -> none  [the longest x1 86 us: per_device(): lax.all_to_all(copies_rows, 'expert', split_axis=0, concat_axis=0, tiled=...]
    ppermute x18 -> x0, starting transfers between devices: 127 us -> none  [swapped(): return lax.ppermute(block, axis, route)]
    dot_general x14 -> x1, matrix products: 37.6 us -> 0.77 us  [per_device(): jnp.einsum('ect,te->ec', place, chosen, precision=highest).reshape(-1, 1)]
    all_to_all x4 -> x0, starting transfers between devices: 34.2 us -> none  [the longest x1 13 us: per_device(): lax.all_to_all(copies_rows, 'expert', split_axis=0, concat_axis=0, tiled=...]
    unnamed x32 -> x13, local copies, waits for them, and re-layouts: 0.64 us -> 8.16 us
  transfers between devices with their start and end apart: 22 -> 0, of which waited for: 15 -> 0; matrix products, arithmetic and copies ran while one was open for 5% -> 0% of each run, Pallas kernels for 0% -> 0%
where the time goes in v1:
time: 194 us; the launch traced here: 193 us
  Pallas kernels  182 us (94%)
  local copies, waits for them, and re-layouts  8.42 us (4%)
    pallas_call x1, Pallas kernels, per_device(): pl.pallas_call(kernel, out_shape=(jax.ShapeDtypeStruct((tok_count, width)...  182 us
    unnamed x13, local copies, waits for them, and re-layouts  8.16 us

profile of v1, /device:TPU:33, one launch (start us, length us, event | category | flops | bytes accessed | tf_op | source)
XLA Modules:
  0.0 193.4 jit_solution(9165445777981713895)
XLA Ops:
  0.6 0.1 eq.43
  0.7 0.7 select_reduce_fusion
  1.4 0.1 copy.17
  1.6 0.2 reduce_window_sum.11
  1.7 0.1 copy.18
  1.8 0.7 fusion.place_hbm
  2.5 0.8 convolution_bitcast_fusion.gsl_hbm
  3.3 181.9 %shard_map.110 = (bf16[128,7168]{1,0:T(8,128)(2,1)}, bf16[128,7168]{1,0:T(8,128)(2,1)}, bf16[3584,128]{1,0:T(8,128)(2,1)}, bf16[3584,128]{1,0:T(8,128)(2,1)}, bf16[128,3584]{1,0:T(8,128)(2,1)}) custom-call(bf16[128,7168]{1,0:T(8,128)(2,1)} %tok_hbm.1, bf16[128,7168]{1,0:T(8,128)(2,1)} %cot_hbm.1, bf16[32,128]{1,0:T(8,128)(2,1)} %fusion.place_hbm, ...), custom_call_target="tpu_custom_call" | custom-call | tf_op jit(solution)/shard_map/pallas_call | solution.py:402
  185.2 0.0 copy-start
  185.2 3.0 %copy.27 = bf16[128,7168]{1,0:T(8,128)(2,1)} copy(bf16[128,7168]{1,0:T(8,128)(2,1)} %get-tuple-element.22) | data formatting | bytes 3670016
  188.2 0.0 copy-done
  188.2 0.0 copy-start.3
  188.2 1.2 copy.28
  189.4 0.6 copy-done.3
  190.0 0.0 copy-start.2
  190.0 0.0 copy-start.1
  190.0 0.9 copy.29
  190.9 0.6 copy-done.2
  191.5 0.9 copy.30
  192.4 0.0 copy-done.1
  192.4 0.9 copy.31
  (2 shorter events, 0.0 us)
Async XLA Ops:
  185.2 3.0 %copy-start = (bf16[128,7168]{1,0:T(8,128)(2,1)S(1)}, bf16[128,7168]{1,0:T(8,128)(2,1)}, u32[]{:S(2)}) copy-start(bf16[128,7168]{1,0:T(8,128)(2,1)} %get-tuple-element.23) | copy-start | bytes 5505028
  188.2 1.8 copy-start.3
  190.0 1.5 copy-start.2
  190.0 2.4 %copy-start.1 = (bf16[128,3584]{1,0:T(8,128)(2,1)S(1)}, bf16[128,3584]{1,0:T(8,128)(2,1)}, u32[]{:S(2)}) copy-start(bf16[128,3584]{1,0:T(8,128)(2,1)} %get-tuple-element.14) | copy-start | bytes 2752516

commit v2 on v1

--- a/solution.py
+++ b/solution.py
@@ -7,7 +7,6 @@
 from jax.experimental.pallas import tpu as pltpu
 from jax.sharding import PartitionSpec as P
 
-GROUP = 8
 CAP = 8
 NY = 4
 NX = 4
@@ -18,15 +17,20 @@
 BF16 = jnp.bfloat16
 
 
-def route_tables(expert_ids, gate_weights, flight):
-    experts = jnp.arange(flight, dtype=jnp.int32)
-    match = (expert_ids[:, :, None] == experts).astype(F32)
-    hits = jnp.sum(match, axis=1)
-    chosen = jnp.sum(match * gate_weights[:, :, None], axis=1)
-    slots = jnp.cumsum(hits, axis=0) - 1.0
-    levels = jnp.arange(CAP, dtype=F32)
-    place = hits.T[:, None, :] * (slots.T[:, None, :] == levels[None, :, None]).astype(F32)
-    return place, chosen
+def route(ids, gates):
+    count = ids.shape[1]
+    hits, chosen = [], []
+    for expert in range(NY):
+        match = ids == expert
+        hits.append(jnp.sum(match.astype(F32), axis=0, keepdims=True))
+        chosen.append(jnp.sum(jnp.where(match, gates, 0.0), axis=0, keepdims=True))
+    tri = lax.broadcasted_iota(jnp.int32, (count, count), 0) <= lax.broadcasted_iota(jnp.int32, (count, count), 1)
+    stacked = jnp.concatenate([jnp.broadcast_to(hit, (CAP, count)) for hit in hits], axis=0)
+    slots = dot(stacked.astype(BF16), tri.astype(F32).astype(BF16)) - 1.0
+    level = lax.rem(lax.broadcasted_iota(jnp.int32, (NY * CAP, count), 0), CAP).astype(F32)
+    place = jnp.where(slots == level, stacked, 0.0)
+    gate = jnp.concatenate([jnp.broadcast_to(row, (CAP, count)) for row in chosen], axis=0)
+    return place, jnp.sum(place * gate, axis=1, keepdims=True)
 
 
 def dot(a, b):
@@ -42,10 +46,10 @@
 
 
 def kernel(
-    tok_hbm, cot_hbm, place_hbm, gsl_hbm, wg_hbm, wu_hbm, wd_hbm,
-    mixed_hbm, igrad_hbm, gg_hbm, gu_hbm, gd_hbm,
-    tok, cot, place, gsl, wgu, wguT, wd, wdT, sb, xs, x2d, s2d, part, pbs, pbr,
-    h16, dgu16, ob, mid, rb, fb, mixed, igrad, gg, gu, gd,
+    tok_hbm, cot_hbm, ids_hbm, gates_hbm, wg_hbm, wu_hbm, wd_hbm,
+    fb, gg_hbm, gu_hbm, gd_hbm,
+    tok, cot, ids, gates, place, gsl, wgu, wguT, wd, wdT, sb, xs, x2d, s2d, part, pbs, pbr,
+    h16, dgu16, ob, mid, rb, gg, gu, gd,
     in_sem, out_sem, zsend, xsend, xfsend, recv, psend, precv, msend, mrecv, rsend, rrecv, osend, orecv,
 ):
     half = wd.shape[1]
@@ -97,8 +101,8 @@
     pl.semaphore_signal(barrier, inc=1, device_id=(p, yz + left), device_id_type=MESH)
 
     loads = [
-        pltpu.make_async_copy(place_hbm, place, in_sem.at[0]),
-        pltpu.make_async_copy(gsl_hbm, gsl, in_sem.at[1]),
+        pltpu.make_async_copy(ids_hbm, ids, in_sem.at[0]),
+        pltpu.make_async_copy(gates_hbm, gates, in_sem.at[1]),
         pltpu.make_async_copy(tok_hbm, tok, in_sem.at[2]),
         pltpu.make_async_copy(cot_hbm, cot, in_sem.at[3]),
         pltpu.make_async_copy(wg_hbm, wgu.at[:, pl.ds(0, 128)], in_sem.at[4]),
@@ -107,7 +111,12 @@
     ]
     for load in loads:
         load.start()
-    for load in loads[:4]:
+    for load in loads[:2]:
+        load.wait()
+    placed, gate_slot = route(ids[...], gates[...])
+    place[...] = placed.astype(BF16)
+    gsl[...] = gate_slot
+    for load in loads[2:4]:
         load.wait()
 
     def slot_rows(ct):
@@ -272,7 +281,6 @@
         loop(4, one)
 
     send_out(0)
-    send_out(1)
     for load in loads[4:]:
         load.wait()
 
@@ -283,53 +291,58 @@
 
     loop(tiles, turn)
     gather_own(0)
-
-    def weight_grads():
+    send_out(1)
+
+    def weight_grads(first, last):
         dguT = dgu16[...].T
         hT = h16[...].T
 
-        def tile(ct):
-            cols = pl.ds(pl.multiple_of(ct * TILE, TILE), TILE)
+        def tile(n):
+            cols = pl.ds(pl.multiple_of((n + first) * TILE, TILE), TILE)
             both = dot(dguT, x2d[:, cols]).T
             gg[cols, :] = both[:, 0:128].astype(BF16)
             gu[cols, :] = both[:, 128:256].astype(BF16)
             gd[:, cols] = dot(hT, s2d[:, cols]).astype(BF16)
 
-        loop(tiles, tile)
+        loop(last - first, tile)
 
     def turn_of(i):
+        @pl.when(i < 4)
+        def _():
+            gather_forward(i)
+
+        @pl.when(i < 3)
+        def _():
+            gather_own(i + 1)
+
         @pl.when(i < 2)
         def _():
             send_out(i + 2)
 
-        @pl.when(i < 4)
-        def _():
-            gather_forward(i)
-
-        @pl.when(i < 3)
-        def _():
-            gather_own(i + 1)
+        @pl.when(i >= 2)
+        def _():
+            add_mid(i - 2)
+
+        @pl.when(jnp.logical_and(i >= 1, i < 5))
+        def _():
+            second_dots(i - 1)
 
         @pl.when(i < 4)
         def _():
             gather_rest(i)
             first_dots(i)
 
+        @pl.when(i == 5)
+        def _():
+            weight_grads(4, tiles)
+
         @pl.when(i >= 2)
         def _():
-            add_mid(i - 2)
-
-        @pl.when(jnp.logical_and(i >= 1, i < 5))
-        def _():
-            second_dots(i - 1)
-
-        @pl.when(i >= 2)
-        def _():
             add_last(i - 2)
 
         @pl.when(i == 4)
         def _():
-            weight_grads()
+            weight_grads(0, 4)
 
     loop(6, turn_of)
 
@@ -337,34 +350,8 @@
         pltpu.make_async_copy(gg, gg_hbm, out_sem.at[0]),
         pltpu.make_async_copy(gu, gu_hbm, out_sem.at[1]),
         pltpu.make_async_copy(gd, gd_hbm, out_sem.at[2]),
-        pltpu.make_async_copy(mixed, mixed_hbm, out_sem.at[3]),
-        pltpu.make_async_copy(igrad, igrad_hbm, out_sem.at[4]),
     ]
-    for store in stores[:3]:
-        store.start()
-
-    def landed(t):
-        k, hz = lax.div(t, 4), lax.rem(t, 4)
-        hh, zz = lax.div(hz, 2), lax.rem(hz, 2)
-        arrived(fb.at[k, hh, zz], orecv.at[t])
-
-    loop(16, landed)
-
-    placeT = place[...].T
-
-    def combine(ct):
-        hf, col = lax.div(ct, tiles), lax.rem(ct, tiles) * TILE
-        cols = pl.ds(pl.multiple_of(ct * TILE, TILE), TILE)
-        fr = pl.ds(pl.multiple_of(col, TILE), TILE)
-
-        def both(k):
-            return (fb[:, hf, 0, k, :, fr].astype(F32) + fb[:, hf, 1, k, :, fr].astype(F32)).reshape(32, TILE)
-
-        mixed[:, cols] = dot(placeT, (both(0) * gsl[...]).astype(BF16)).astype(BF16)
-        igrad[:, cols] = dot(placeT, both(1).astype(BF16)).astype(BF16)
-
-    loop(2 * tiles, combine)
-    for store in stores[3:]:
+    for store in stores:
         store.start()
 
     loop(15, lambda t: zcopy(t + 1).wait_send())
@@ -383,18 +370,60 @@
 
     loop(16, sent)
     loop(STAGES, lambda i: pcopy(i).wait_send())
+
+    def landed(t):
+        k, hz = lax.div(t, 4), lax.rem(t, 4)
+        hh, zz = lax.div(hz, 2), lax.rem(hz, 2)
+        arrived(fb.at[k, hh, zz], orecv.at[t])
+
+    loop(16, landed)
     for store in stores:
         store.wait()
 
 
+def finish(
+    ids_ref, gates_ref, fb_hbm, gg_in, gu_in, gd_in, mixed_hbm, igrad_hbm, gg_out, gu_out, gd_out,
+    fb, mixed, igrad, gg, gu, gd, in_sem, out_sem, pass_sem,
+):
+    half = fb.shape[-1]
+    grads = ((gg_in, gg, gg_out), (gu_in, gu, gu_out), (gd_in, gd, gd_out))
+    enter = [pltpu.make_async_copy(grad[0], grad[1], pass_sem.at[0, n]) for n, grad in enumerate(grads)]
+    leave = [pltpu.make_async_copy(grad[1], grad[2], pass_sem.at[1, n]) for n, grad in enumerate(grads)]
+    fetch = [pltpu.make_async_copy(fb_hbm.at[:, hf], fb.at[:, hf], in_sem.at[hf]) for hf in range(2)]
+    for copy in fetch + enter:
+        copy.start()
+    place, gsl = route(ids_ref[...], gates_ref[...])
+    placeT = place.T.astype(BF16)
+    stores = []
+    for hf in range(2):
+        fetch[hf].wait()
+        for col in range(0, half, TILE):
+            fr, to = pl.ds(col, TILE), pl.ds(hf * half + col, TILE)
+
+            def both(k):
+                return (fb[:, hf, 0, k, :, fr].astype(F32) + fb[:, hf, 1, k, :, fr].astype(F32)).reshape(32, TILE)
+
+            mixed[:, to] = dot(placeT, (both(0) * gsl).astype(BF16)).astype(BF16)
+            igrad[:, to] = dot(placeT, both(1).astype(BF16)).astype(BF16)
+        if hf == 0:
+            for get, put in zip(enter, leave):
+                get.wait()
+                put.start()
+        cols = pl.ds(hf * half, half)
+        stores += [
+            pltpu.make_async_copy(mixed.at[:, cols], mixed_hbm.at[:, cols], out_sem.at[hf, 0]),
+            pltpu.make_async_copy(igrad.at[:, cols], igrad_hbm.at[:, cols], out_sem.at[hf, 1]),
+        ]
+        stores[-2].start()
+        stores[-1].start()
+    for copy in stores + leave:
+        copy.wait()
+
+
 def per_device(tokens, cotangent, expert_ids, gate_weights, w_gate, w_up, w_down):
-    flight = lax.axis_size("expert") // GROUP
     tok_count, width = tokens.shape
     half = width // 2
-    highest = lax.Precision.HIGHEST
-    place, chosen = route_tables(expert_ids, gate_weights, flight)
-    gate_slot = jnp.einsum("ect,te->ec", place, chosen, precision=highest).reshape(-1, 1)
-    place16 = place.reshape(flight * CAP, tok_count).astype(BF16)
+    ids, gates = expert_ids.T, gate_weights.T
     dma = pltpu.SemaphoreType.DMA
     vmem = pltpu.VMEM
     piece = (2, CAP, half)
@@ -402,17 +431,18 @@
     outs = pl.pallas_call(
         kernel,
         out_shape=(
-            jax.ShapeDtypeStruct((tok_count, width), BF16),
-            jax.ShapeDtypeStruct((tok_count, width), BF16),
+            jax.ShapeDtypeStruct((NY, 2, 2) + piece, BF16),
             jax.ShapeDtypeStruct((half, 128), BF16),
             jax.ShapeDtypeStruct((half, 128), BF16),
             jax.ShapeDtypeStruct((128, half), BF16),
         ),
         in_specs=[any_spec] * 7,
-        out_specs=[any_spec] * 5,
+        out_specs=[any_spec] * 4,
         scratch_shapes=[
             vmem((tok_count, width), BF16),
             vmem((tok_count, width), BF16),
+            vmem(ids.shape, jnp.int32),
+            vmem(gates.shape, F32),
             vmem((32, tok_count), BF16),
             vmem((32, 1), F32),
             vmem((half, 256), BF16),
@@ -431,14 +461,11 @@
             vmem((NX, 16) + piece, BF16),
             vmem((16,) + piece, BF16),
             vmem((2, 16) + piece, BF16),
-            vmem((NY, 2, 2) + piece, BF16),
-            vmem((tok_count, width), BF16),
-            vmem((tok_count, width), BF16),
             vmem((half, 128), BF16),
             vmem((half, 128), BF16),
             vmem((128, half), BF16),
             dma((7,)),
-            dma((5,)),
+            dma((3,)),
             dma((16,)),
             dma((2, 16)),
             dma((16,)),
@@ -455,8 +482,33 @@
         compiler_params=pltpu.CompilerParams(
             collective_id=0, has_side_effects=True, vmem_limit_bytes=60 * 1024 * 1024
         ),
-    )(tokens, cotangent, place16, gate_slot, w_gate[0], w_up[0], w_down[0])
-    return outs[0], outs[1], outs[2][None], outs[3][None], outs[4][None]
+    )(tokens, cotangent, ids, gates, w_gate[0], w_up[0], w_down[0])
+    whole = pl.BlockSpec(memory_space=vmem)
+    mixed, igrad, gg, gu, gd = pl.pallas_call(
+        finish,
+        out_shape=(
+            jax.ShapeDtypeStruct((tok_count, width), BF16),
+            jax.ShapeDtypeStruct((tok_count, width), BF16),
+            jax.ShapeDtypeStruct((half, 128), BF16),
+            jax.ShapeDtypeStruct((half, 128), BF16),
+            jax.ShapeDtypeStruct((128, half), BF16),
+        ),
+        in_specs=[whole] * 2 + [any_spec] * 4,
+        out_specs=[any_spec] * 5,
+        scratch_shapes=[
+            vmem((NY, 2, 2) + piece, BF16),
+            vmem((tok_count, width), BF16),
+            vmem((tok_count, width), BF16),
+            vmem((half, 128), BF16),
+            vmem((half, 128), BF16),
+            vmem((128, half), BF16),
+            dma((2,)),
+            dma((2, 2)),
+            dma((2, 3)),
+        ],
+        compiler_params=pltpu.CompilerParams(vmem_limit_bytes=60 * 1024 * 1024),
+    )(ids, gates, *outs)
+    return mixed, igrad, gg[None], gu[None], gd[None]
 
 
 def solution(mesh):

time: 194 us -> 178 us (0.918)
  local copies, waits for them, and re-layouts: 8.42 us -> 0 us
  Pallas kernels: 182 us -> 177 us
    unnamed x13 -> x0, local copies, waits for them, and re-layouts: 8.16 us -> none
    pallas_call x1 -> x2, Pallas kernels: 182 us -> 177 us  [the longest x1 171 us: per_device(): pl.pallas_call(kernel, out_shape=(jax.ShapeDtypeStruct((NY, 2, 2) + piece...]
where the time goes in v2:
time: 178 us; the launch traced here: 177 us
  Pallas kernels  177 us (99%)
    pallas_call x1, Pallas kernels, per_device(): pl.pallas_call(kernel, out_shape=(jax.ShapeDtypeStruct((NY, 2, 2) + piece...  171 us
    pallas_call x1, Pallas kernels, per_device(): pl.pallas_call(finish, out_shape=(jax.ShapeDtypeStruct((tok_count, width)...  5.61 us

profile of v2, /device:TPU:33, one launch (start us, length us, event | category | flops | bytes accessed | tf_op | source)
XLA Modules:
  0.0 177.4 jit_solution(15299868402854114644)
XLA Ops:
  0.6 171.1 %shard_map.110 = (bf16[4,2,2,2,8,3584]{5,4,3,2,1,0:T(8,128)(2,1)}, bf16[3584,128]{1,0:T(8,128)(2,1)}, bf16[3584,128]{1,0:T(8,128)(2,1)}, bf16[128,3584]{1,0:T(8,128)(2,1)}) custom-call(bf16[128,7168]{1,0:T(8,128)(2,1)} %tok_hbm.1, bf16[128,7168]{1,0:T(8,128)(2,1)} %cot_hbm.1, s32[8,128]{1,0:T(8,128)} %bitcast.11, f32[8,128]{1,0:T(8,128)} %bitcast.13, ...), custom_call_target="tpu_custom_call" | custom-call | tf_op jit(solution)/shard_map/pallas_call | solution.py:431
  171.8 5.6 %shard_map.111 = (bf16[128,7168]{1,0:T(8,128)(2,1)}, bf16[128,7168]{1,0:T(8,128)(2,1)}, bf16[3584,128]{1,0:T(8,128)(2,1)}, bf16[3584,128]{1,0:T(8,128)(2,1)}, bf16[128,3584]{1,0:T(8,128)(2,1)}) custom-call(s32[8,128]{1,0:T(8,128)} %bitcast.12, f32[8,128]{1,0:T(8,128)} %bitcast.14, bf16[4,2,2,2,8,3584]{5,4,3,2,1,0:T(8,128)(2,1)} %get-tuple-element.14.fb_hbm, ...), custom_call_target="tpu_custom_call" | custom-call | tf_op jit(solution)/shard_map/pallas_call | solution.py:487

commit v3 on v2

v3 whole, which is shorter than its diff:
```python
import jax
import jax.numpy as jnp
from jax import lax
from jax.experimental import pallas as pl
from jax.experimental.pallas import tpu as pltpu
from jax.sharding import PartitionSpec as P

CAP = 8
NY = 4
NX = 4
STAGES = 4
WIDE = 896
NARROW = 256
MESH = pl.DeviceIdType.MESH
F32 = jnp.float32
BF16 = jnp.bfloat16


def dot(a, b):
    return jnp.dot(a, b, preferred_element_type=F32)


def loop(n, body):
    def step(i, carry):
        body(i)
        return carry

    lax.fori_loop(0, n, step, 0)


def span(start, size):
    return pl.ds(pl.multiple_of(start, 128), size)


def route(ids, gates):
    count = ids.shape[1]
    hits, chosen = [], []
    for expert in range(NY):
        match = ids == expert
        hits.append(jnp.sum(match.astype(F32), axis=0, keepdims=True))
        chosen.append(jnp.sum(jnp.where(match, gates, 0.0), axis=0, keepdims=True))
    tri = lax.broadcasted_iota(jnp.int32, (count, count), 0) <= lax.broadcasted_iota(jnp.int32, (count, count), 1)
    stacked = jnp.concatenate([jnp.broadcast_to(hit, (CAP, count)) for hit in hits], axis=0)
    slots = dot(stacked.astype(BF16), tri.astype(F32).astype(BF16)) - 1.0
    level = lax.rem(lax.broadcasted_iota(jnp.int32, (NY * CAP, count), 0), CAP).astype(F32)
    place = jnp.where(slots == level, stacked, 0.0)
    gate = jnp.concatenate([jnp.broadcast_to(row, (CAP, count)) for row in chosen], axis=0)
    return place, jnp.sum(place * gate, axis=1, keepdims=True)


def kernel(
    tok_hbm, cot_hbm, ids_hbm, gates_hbm, wg_hbm, wu_hbm, wd_hbm,
    fb, gg_hbm, gu_hbm, gd_hbm,
    tok, cot, ids, gates, place, gsl, wcat, wcatT, wd, wdT, sb, xs, x2d, s2d, part, own_send, own_recv,
    pair_send, pair_recv, hb, h16, dgu16, ob, rb, gg, gu, gd,
    in_sem, wsend, wrecv, zsend, recv, fsend, asend, arecv, bsend, brecv, hsend, hrecv,
    rsend, rrecv, osend, orecv, gsend, grecv, gown,
):
    quarter = wd.shape[1]
    p = lax.axis_index("pipe")
    e = lax.axis_index("expert")
    y = lax.div(e, 8)
    zh = lax.rem(lax.div(e, 4), 2)
    x = lax.rem(e, 4)
    yz = e - x
    h = lax.div(p, 4)
    q = p + h * (7 - 2 * p)
    shift = lax.rem(q, 2)
    u = lax.rem(x + 3 * shift, 4)
    role = lax.div(lax.rem(u + 1, 4), 2)
    other = 1 - role
    partner = lax.rem(u + 1 - 2 * lax.rem(u, 2) + shift, 4)
    twin = lax.rem(3 - u + shift, 4)
    across = lax.rem(x + 2, 4)
    inner = lax.div(lax.rem(lax.div(p, 2) + 1, 4), 2)
    gid = h * 2 + zh

    def rank_of(hh):
        return q + hh * (7 - 2 * q)

    def place_of(d):
        hh = lax.rem(h + lax.div(d, 2), 2)
        zz = lax.rem(zh + lax.rem(d, 2), 2)
        return hh, zz

    nearest = (0, 3 - inner, 2 + inner, 1)

    def remote(src, dst, ssem, rsem, rank, expert):
        return pltpu.make_async_remote_copy(
            src_ref=src, dst_ref=dst, send_sem=ssem, recv_sem=rsem,
            device_id=(rank, expert), device_id_type=MESH)

    def arrived(ref, sem):
        pltpu.make_async_copy(ref, ref, sem).wait()

    barrier = pltpu.get_barrier_semaphore()

    def greet(t):
        j, d, side = lax.div(t, 8), lax.rem(lax.div(t, 2), 4), lax.rem(t, 2)
        hh, zz = place_of(d)
        xx = x + side * (partner - x)
        pl.semaphore_signal(
            barrier, inc=1, device_id=(rank_of(hh), lax.rem(y + j, 4) * 8 + zz * 4 + xx), device_id_type=MESH)

    loop(31, lambda t: greet(t + 1))
    pl.semaphore_signal(barrier, inc=1, device_id=(p, yz + twin), device_id_type=MESH)

    mine, theirs = span(role * quarter, quarter), span(other * quarter, quarter)
    gate_cols, up_cols, down_rows = span(role * 256, 128), span(role * 256 + 128, 128), span(role * 128, 128)
    loads = [
        pltpu.make_async_copy(ids_hbm, ids, in_sem.at[0]),
        pltpu.make_async_copy(gates_hbm, gates, in_sem.at[1]),
        pltpu.make_async_copy(tok_hbm, tok, in_sem.at[2]),
        pltpu.make_async_copy(cot_hbm, cot, in_sem.at[3]),
        pltpu.make_async_copy(wg_hbm.at[mine, :], wcat.at[:, gate_cols], in_sem.at[4]),
        pltpu.make_async_copy(wu_hbm.at[mine, :], wcat.at[:, up_cols], in_sem.at[5]),
        pltpu.make_async_copy(wd_hbm.at[:, mine], wd.at[down_rows, :], in_sem.at[6]),
    ]
    weights = [
        remote(wg_hbm.at[theirs, :], wcat.at[:, gate_cols], wsend.at[0], wrecv.at[0], p, yz + partner),
        remote(wu_hbm.at[theirs, :], wcat.at[:, up_cols], wsend.at[1], wrecv.at[1], p, yz + partner),
        remote(wd_hbm.at[:, theirs], wd.at[down_rows, :], wsend.at[2], wrecv.at[2], p, yz + partner),
    ]
    for load in loads:
        load.start()
    for load in loads[:2]:
        load.wait()
    placed, gate_slot = route(ids[...], gates[...])
    place[...] = placed.astype(BF16)
    gsl[...] = gate_slot
    for load in loads[2:4]:
        load.wait()

    def slot_rows(ct):
        k, col = lax.div(ct, 2), lax.rem(ct, 2)
        hf, ro = lax.div(k, 2), lax.rem(k, 2)
        cols, to = span(ct * WIDE, WIDE), span(col * WIDE, WIDE)
        rows = dot(place[...], tok[:, cols])
        sb[:, hf, ro, 0, :, to] = rows.reshape(NY, CAP, WIDE).astype(BF16)
        raw = dot(place[...], cot[:, cols]) * gsl[...]
        sb[:, hf, ro, 1, :, to] = raw.reshape(NY, CAP, WIDE).astype(BF16)

    loop(8, slot_rows)
    pl.semaphore_wait(barrier, 32)

    own_s = y * 4 + gid
    local = pltpu.make_async_copy(sb.at[y, h, role], xs.at[x, own_s], recv.at[x, own_s])

    def zcopy(i, d, side):
        hh, zz = place_of(d)
        yy = lax.rem(y + 4 - i, 4)
        ro = role + side * (1 - 2 * role)
        xx = partner if side else x
        return remote(sb.at[yy, hh, ro], xs.at[x, own_s], zsend.at[i, d, side], recv.at[x, own_s],
                      rank_of(hh), yy * 8 + zz * 4 + xx)

    def send_out(i):
        for d in nearest[:0:-1]:
            zcopy(i, d, 0).start()
            zcopy(i, d, 1).start()
        zcopy(i, 0, 1).start()

        @pl.when(i == 0)
        def _():
            local.start()

        @pl.when(i > 0)
        def _():
            zcopy(i, 0, 0).start()

    def base(i):
        return lax.rem(y + i, 4) * 4

    def source(i, d):
        hh, zz = place_of(d)
        return base(i) + hh * 2 + zz

    def fcopy(s, side):
        c = partner if side else x
        return remote(xs.at[c, s], xs.at[c, s], fsend.at[side, s], recv.at[c, s], p, yz + twin)

    def forward(i):
        for d in nearest:
            s = source(i, d)
            for side, c in ((0, x), (1, partner)):
                arrived(xs.at[c, s], recv.at[c, s])
                fcopy(s, side).start()

    def rows_of(i):
        return span(i * 128, 128)

    def acopy(i):
        return remote(own_send.at[i], own_recv.at[i], asend.at[i], arecv.at[i], p, yz + partner)

    def bcopy(i):
        return remote(pair_send.at[i], pair_recv.at[i], bsend.at[i], brecv.at[i], 7 - p, e)

    def hcopy(i):
        return remote(hb.at[i, role], hb.at[i, role], hsend.at[i], hrecv.at[i], p, yz + partner)

    def first_dots(i):
        def rest(j):
            s = base(i) + j
            arrived(xs.at[twin, s], recv.at[twin, s])
            arrived(xs.at[across, s], recv.at[across, s])

        loop(4, rest)

        def flatten(c):
            to = pl.ds(pl.multiple_of(i * 128 + c * 32, 32), 32)
            x2d[to, :] = xs[c, pl.ds(base(i), 4), 0].astype(F32).reshape(32, quarter).astype(BF16)
            s2d[to, :] = xs[c, pl.ds(base(i), 4), 1].astype(F32).reshape(32, quarter).astype(BF16)

        loop(4, flatten)
        rows = rows_of(i)
        pre = dot(x2d[rows, :], wcat[...])
        dh = dot(s2d[rows, :], wdT[...])
        for k in range(2):
            part[i, k, :, 0:256] = pre[:, k * 256:k * 256 + 256]
            part[i, k, :, 256:384] = dh[:, k * 128:k * 128 + 128]
        own_send[i] = part[i, other].reshape(16, 8, 384).astype(BF16)
        acopy(i).start()

    def add_partner(i):
        arrived(own_recv.at[i], arecv.at[i])
        both = part[i, role] + own_recv[i].astype(F32).reshape(128, 384)
        part[i, role] = both
        pair_send[i] = both.reshape(16, 8, 384).astype(BF16)
        bcopy(i).start()

    def activate(i):
        arrived(pair_recv.at[i], brecv.at[i])
        whole = part[i, role] + pair_recv[i].astype(F32).reshape(128, 384)
        gate, up, dh = whole[:, 0:128], whole[:, 128:256], whole[:, 256:384]
        sigma = jax.nn.sigmoid(gate)
        active = gate * sigma
        hb[i, role, :, :, 0:128] = (active * up).reshape(16, 8, 128).astype(BF16)
        dgate = dh * up * sigma * (1.0 + gate * (1.0 - sigma))
        hb[i, role, :, :, 128:256] = dgate.reshape(16, 8, 128).astype(BF16)
        hb[i, role, :, :, 256:384] = (dh * active).reshape(16, 8, 128).astype(BF16)
        hcopy(i).start()

    def rcopy(s, side):
        c = across if side else twin
        return remote(ob.at[c, s], rb.at[side, s], rsend.at[side, s], rrecv.at[side, s], p, yz + twin)

    def second_dots(i):
        rows = rows_of(i)
        arrived(hb.at[i, other], hrecv.at[i])
        for k in range(2):
            flat = hb[i, k].astype(F32).reshape(128, 384).astype(BF16)
            h16[rows, k * 128:k * 128 + 128] = flat[:, 0:128]
            dgu16[rows, k * 256:k * 256 + 256] = flat[:, 128:384]

        def tile(ct):
            cols = span(ct * WIDE, WIDE)
            out = dot(h16[rows, :], wd[:, cols])
            ob[:, pl.ds(base(i), 4), 0, :, cols] = out.reshape(NX, 4, CAP, WIDE).astype(BF16)
            back = dot(dgu16[rows, :], wcatT[:, cols])
            ob[:, pl.ds(base(i), 4), 1, :, cols] = back.reshape(NX, 4, CAP, WIDE).astype(BF16)

        loop(2, tile)
        for d in nearest[::-1]:
            s = source(i, d)
            rcopy(s, 0).start()
            rcopy(s, 1).start()

    def seat(hf, ro, zz):
        return (hf * 2 + ro) * 2 + zz

    def ocopy(i, d, side):
        hh, zz = place_of(d)
        yy = lax.rem(y + i, 4)
        s = source(i, d)
        c = partner if side else x
        return remote(ob.at[c, s], fb.at[y, seat(h, role, zh)], osend.at[side, s], orecv.at[y, seat(h, role, zh)],
                      rank_of(hh), yy * 8 + zz * 4 + c)

    own_out = pltpu.make_async_copy(ob.at[x, own_s], fb.at[y, seat(h, role, zh)], orecv.at[y, seat(h, role, zh)])

    def add_twin(i):
        for d in nearest[::-1]:
            s = source(i, d)
            for side, c in ((0, x), (1, partner)):
                arrived(rb.at[side, s], rrecv.at[side, s])
                ob[c, s] = (ob[c, s].astype(F32) + rb[side, s].astype(F32)).astype(BF16)
                if side == 1 or d is not nearest[0]:
                    ocopy(i, d, side).start()
                    continue

                @pl.when(i == 0)
                def _():
                    own_out.start()

                @pl.when(i > 0)
                def _():
                    ocopy(i, d, side).start()

    def weight_grads(k):
        dguT = dgu16[:, span(k * 256, 256)].T
        hT = h16[:, span(k * 128, 128)].T

        def tile(ct):
            cols = span(ct * NARROW, NARROW)
            both = dot(dguT, x2d[:, cols]).T
            gg[k, cols, :] = both[:, 0:128].astype(BF16)
            gu[k, cols, :] = both[:, 128:256].astype(BF16)
            gd[k, :, cols] = dot(hT, s2d[:, cols]).astype(BF16)

        loop(quarter // NARROW, tile)

    grads_away = [
        remote(gg.at[other], gg_hbm.at[mine, :], gsend.at[0], grecv.at[0], p, yz + partner),
        remote(gu.at[other], gu_hbm.at[mine, :], gsend.at[1], grecv.at[1], p, yz + partner),
        remote(gd.at[other], gd_hbm.at[:, mine], gsend.at[2], grecv.at[2], p, yz + partner),
    ]
    grads_own = [
        pltpu.make_async_copy(gg.at[role], gg_hbm.at[mine, :], gown.at[0]),
        pltpu.make_async_copy(gu.at[role], gu_hbm.at[mine, :], gown.at[1]),
        pltpu.make_async_copy(gd.at[role], gd_hbm.at[:, mine], gown.at[2]),
    ]

    send_out(0)
    for copy in weights:
        copy.start()
    forward(0)
    send_out(1)
    for load in loads[4:]:
        load.wait()
    for copy in weights:
        copy.wait_recv()

    def turn(ct):
        cols = span(ct * NARROW, NARROW)
        wcatT[:, cols] = wcat[cols, :].T
        wdT[cols, :] = wd[:, cols].T

    loop(quarter // NARROW, turn)

    def turn_of(i):
        @pl.when(i < 4)
        def _():
            first_dots(i)

        @pl.when(jnp.logical_and(i >= 1, i < 5))
        def _():
            activate(i - 1)

        @pl.when(i < 3)
        def _():
            forward(i + 1)

        @pl.when(i < 2)
        def _():
            send_out(i + 2)

        @pl.when(i < 4)
        def _():
            add_partner(i)

        @pl.when(jnp.logical_and(i >= 1, i < 5))
        def _():
            second_dots(i - 1)

        @pl.when(i == 4)
        def _():
            weight_grads(other)
            for copy in grads_away:
                copy.start()

        @pl.when(i >= 2)
        def _():
            add_twin(i - 2)

    loop(6, turn_of)
    weight_grads(role)
    for copy in grads_own:
        copy.start()

    for copy in weights + grads_away:
        copy.wait_send()
    for i in range(STAGES):
        for side in range(2):
            for d in range(4):
                if (i, d, side) != (0, 0, 0):
                    zcopy(i, d, side).wait_send()

    def sent(i):
        for d in range(4):
            s = source(i, d)
            for side in range(2):
                fcopy(s, side).wait_send()
                rcopy(s, side).wait_send()
                if side == 1 or d > 0:
                    ocopy(i, d, side).wait_send()

        @pl.when(i > 0)
        def _():
            ocopy(i, 0, 0).wait_send()

        acopy(i).wait_send()
        bcopy(i).wait_send()
        hcopy(i).wait_send()

    loop(STAGES, sent)

    def landed(t):
        k, n = lax.div(t, 8), lax.rem(t, 8)
        arrived(fb.at[k, n], orecv.at[k, n])

    loop(32, landed)
    for copy in grads_own:
        copy.wait()
    for copy in grads_away:
        copy.wait_recv()


def finish(
    ids_ref, gates_ref, fb_hbm, gg_in, gu_in, gd_in, mixed_hbm, igrad_hbm, gg_out, gu_out, gd_out,
    fb, mixed, igrad, gg, gu, gd, in_sem, out_sem, pass_sem,
):
    quarter = fb.shape[-1]
    grads = ((gg_in, gg, gg_out), (gu_in, gu, gu_out), (gd_in, gd, gd_out))
    enter = [pltpu.make_async_copy(grad[0], grad[1], pass_sem.at[0, n]) for n, grad in enumerate(grads)]
    leave = [pltpu.make_async_copy(grad[1], grad[2], pass_sem.at[1, n]) for n, grad in enumerate(grads)]
    fetch = [
        pltpu.make_async_copy(fb_hbm.at[:, pl.ds(2 * n, 2)], fb.at[:, pl.ds(2 * n, 2)], in_sem.at[n]) for n in range(4)
    ]
    for copy in fetch + enter:
        copy.start()
    place, gsl = route(ids_ref[...], gates_ref[...])
    placeT = place.T.astype(BF16)
    stores = []
    for n in range(4):
        fetch[n].wait()
        for col in range(0, quarter, WIDE):
            fr, to = pl.ds(col, WIDE), pl.ds(n * quarter + col, WIDE)

            def both(k):
                return (fb[:, 2 * n, k, :, fr].astype(F32) + fb[:, 2 * n + 1, k, :, fr].astype(F32)).reshape(32, WIDE)

            mixed[:, to] = dot(placeT, (both(0) * gsl).astype(BF16)).astype(BF16)
            igrad[:, to] = dot(placeT, both(1).astype(BF16)).astype(BF16)
        if n == 0:
            for get, put in zip(enter, leave):
                get.wait()
                put.start()
        cols = pl.ds(n * quarter, quarter)
        stores += [
            pltpu.make_async_copy(mixed.at[:, cols], mixed_hbm.at[:, cols], out_sem.at[n, 0]),
            pltpu.make_async_copy(igrad.at[:, cols], igrad_hbm.at[:, cols], out_sem.at[n, 1]),
        ]
        stores[-2].start()
        stores[-1].start()
    for copy in stores + leave:
        copy.wait()


def per_device(tokens, cotangent, expert_ids, gate_weights, w_gate, w_up, w_down):
    tok_count, width = tokens.shape
    half, quarter = width // 2, width // 4
    ids, gates = expert_ids.T, gate_weights.T
    dma = pltpu.SemaphoreType.DMA
    vmem = pltpu.VMEM
    piece = (2, CAP, quarter)
    swap = (STAGES, 16, 8, 384)
    any_spec = pl.BlockSpec(memory_space=pl.ANY)
    outs = pl.pallas_call(
        kernel,
        out_shape=(
            jax.ShapeDtypeStruct((NY, 8) + piece, BF16),
            jax.ShapeDtypeStruct((half, 128), BF16),
            jax.ShapeDtypeStruct((half, 128), BF16),
            jax.ShapeDtypeStruct((128, half), BF16),
        ),
        in_specs=[any_spec] * 7,
        out_specs=[any_spec] * 4,
        scratch_shapes=[
            vmem((tok_count, width), BF16),
            vmem((tok_count, width), BF16),
            vmem(ids.shape, jnp.int32),
            vmem(gates.shape, F32),
            vmem((32, tok_count), BF16),
            vmem((32, 1), F32),
            vmem((quarter, 512), BF16),
            vmem((512, quarter), BF16),
            vmem((256, quarter), BF16),
            vmem((quarter, 256), BF16),
            vmem((NY, 2, 2) + piece, BF16),
            vmem((NX, 16) + piece, BF16),
            vmem((512, quarter), BF16),
            vmem((512, quarter), BF16),
            vmem((STAGES, 2, 128, 384), F32),
            vmem(swap, BF16),
            vmem(swap, BF16),
            vmem(swap, BF16),
            vmem(swap, BF16),
            vmem((STAGES, 2, 16, 8, 384), BF16),
            vmem((512, 256), BF16),
            vmem((512, 512), BF16),
            vmem((NX, 16) + piece, BF16),
            vmem((2, 16) + piece, BF16),
            vmem((2, quarter, 128), BF16),
            vmem((2, quarter, 128), BF16),
            vmem((2, 128, quarter), BF16),
            dma((7,)),
            dma((3,)),
            dma((3,)),
            dma((STAGES, 4, 2)),
            dma((NX, 16)),
            dma((2, 16)),
            dma((STAGES,)),
            dma((STAGES,)),
            dma((STAGES,)),
            dma((STAGES,)),
            dma((STAGES,)),
            dma((STAGES,)),
            dma((2, 16)),
            dma((2, 16)),
            dma((2, 16)),
            dma((NY, 8)),
            dma((3,)),
            dma((3,)),
            dma((3,)),
        ],
        compiler_params=pltpu.CompilerParams(
            collective_id=0, has_side_effects=True, vmem_limit_bytes=56 * 1024 * 1024
        ),
    )(tokens, cotangent, ids, gates, w_gate[0], w_up[0], w_down[0])
    whole = pl.BlockSpec(memory_space=vmem)
    mixed, igrad, gg, gu, gd = pl.pallas_call(
        finish,
        out_shape=(
            jax.ShapeDtypeStruct((tok_count, width), BF16),
            jax.ShapeDtypeStruct((tok_count, width), BF16),
            jax.ShapeDtypeStruct((half, 128), BF16),
            jax.ShapeDtypeStruct((half, 128), BF16),
            jax.ShapeDtypeStruct((128, half), BF16),
        ),
        in_specs=[whole] * 2 + [any_spec] * 4,
        out_specs=[any_spec] * 5,
        scratch_shapes=[
            vmem((NY, 8) + piece, BF16),
            vmem((tok_count, width), BF16),
            vmem((tok_count, width), BF16),
            vmem((half, 128), BF16),
            vmem((half, 128), BF16),
            vmem((128, half), BF16),
            dma((4,)),
            dma((4, 2)),
            dma((2, 3)),
        ],
        compiler_params=pltpu.CompilerParams(vmem_limit_bytes=56 * 1024 * 1024),
    )(ids, gates, *outs)
    return mixed, igrad, gg[None], gu[None], gd[None]


def solution(mesh):
    return jax.shard_map(
        per_device,
        mesh=mesh,
        in_specs=(
            P(("pipe", "expert"), None),
            P(("pipe", "expert"), None),
            P(("pipe", "expert"), None),
            P(("pipe", "expert"), None),
            P("pipe", None, "expert"),
            P("pipe", None, "expert"),
            P("pipe", "expert", None),
        ),
        out_specs=(
            P(("pipe", "expert"), None),
            P(("pipe", "expert"), None),
            P("pipe", None, "expert"),
            P("pipe", None, "expert"),
            P("pipe", "expert", None),
        ),
        check_vma=False,
    )
```

time: 178 us -> 147 us (0.83)
  the two profiles are of different devices: /device:TPU:33 before, /device:TPU:67 now
where the time goes in v3:
time: 147 us
  Pallas kernels  146 us (99%)
    pallas_call x1, Pallas kernels, per_device(): pl.pallas_call(kernel, out_shape=(jax.ShapeDtypeStruct((NY, 8) + piece, B...  141 us
    pallas_call x1, Pallas kernels, per_device(): pl.pallas_call(finish, out_shape=(jax.ShapeDtypeStruct((tok_count, width)...  5.25 us

profile of v3, /device:TPU:67, one launch (start us, length us, event | category | flops | bytes accessed | tf_op | source)
XLA Modules:
  0.0 146.7 jit_solution(3304836798875375475)
XLA Ops:
  0.6 140.8 %shard_map.110 = (bf16[4,8,2,8,1792]{4,3,2,1,0:T(8,128)(2,1)}, bf16[3584,128]{1,0:T(8,128)(2,1)}, bf16[3584,128]{1,0:T(8,128)(2,1)}, bf16[128,3584]{1,0:T(8,128)(2,1)}) custom-call(bf16[128,7168]{1,0:T(8,128)(2,1)} %tok_hbm.1, bf16[128,7168]{1,0:T(8,128)(2,1)} %cot_hbm.1, s32[8,128]{1,0:T(8,128)} %bitcast.11, f32[8,128]{1,0:T(8,128)} %bitcast.13, ...), custom_call_target="tpu_custom_call" | custom-call | tf_op jit(solution)/shard_map/pallas_call | solution.py:468
  141.5 5.2 %shard_map.111 = (bf16[128,7168]{1,0:T(8,128)(2,1)}, bf16[128,7168]{1,0:T(8,128)(2,1)}, bf16[3584,128]{1,0:T(8,128)(2,1)}, bf16[3584,128]{1,0:T(8,128)(2,1)}, bf16[128,3584]{1,0:T(8,128)(2,1)}) custom-call(s32[8,128]{1,0:T(8,128)} %bitcast.12, f32[8,128]{1,0:T(8,128)} %bitcast.14, bf16[4,8,2,8,1792]{4,3,2,1,0:T(8,128)(2,1)} %get-tuple-element.14.fb_hbm, ...), custom_call_target="tpu_custom_call" | custom-call | tf_op jit(solution)/shard_map/pallas_call | solution.py:531

commit v4 on v3

--- a/solution.py
+++ b/solution.py
@@ -154,11 +154,18 @@
         return remote(sb.at[yy, hh, ro], xs.at[x, own_s], zsend.at[i, d, side], recv.at[x, own_s],
                       rank_of(hh), yy * 8 + zz * 4 + xx)
 
+    def send_far(i):
+        for d in nearest[:0:-1]:
+            zcopy(i, d, 1).start()
+        zcopy(i, 0, 1).start()
+
     def send_out(i):
+        send_near(i)
+        send_far(i)
+
+    def send_near(i):
         for d in nearest[:0:-1]:
             zcopy(i, d, 0).start()
-            zcopy(i, d, 1).start()
-        zcopy(i, 0, 1).start()
 
         @pl.when(i == 0)
         def _():
@@ -278,23 +285,23 @@
 
     own_out = pltpu.make_async_copy(ob.at[x, own_s], fb.at[y, seat(h, role, zh)], orecv.at[y, seat(h, role, zh)])
 
-    def add_twin(i):
+    def add_twin(i, side):
+        c = partner if side else x
         for d in nearest[::-1]:
             s = source(i, d)
-            for side, c in ((0, x), (1, partner)):
-                arrived(rb.at[side, s], rrecv.at[side, s])
-                ob[c, s] = (ob[c, s].astype(F32) + rb[side, s].astype(F32)).astype(BF16)
-                if side == 1 or d is not nearest[0]:
-                    ocopy(i, d, side).start()
-                    continue
-
-                @pl.when(i == 0)
-                def _():
-                    own_out.start()
-
-                @pl.when(i > 0)
-                def _():
-                    ocopy(i, d, side).start()
+            arrived(rb.at[side, s], rrecv.at[side, s])
+            ob[c, s] = (ob[c, s].astype(F32) + rb[side, s].astype(F32)).astype(BF16)
+            if side == 1 or d is not nearest[0]:
+                ocopy(i, d, side).start()
+                continue
+
+            @pl.when(i == 0)
+            def _():
+                own_out.start()
+
+            @pl.when(i > 0)
+            def _():
+                ocopy(i, d, side).start()
 
     def weight_grads(k):
         dguT = dgu16[:, span(k * 256, 256)].T
@@ -321,10 +328,12 @@
     ]
 
     send_out(0)
+    send_out(1)
+    send_out(2)
+    send_out(3)
     for copy in weights:
         copy.start()
     forward(0)
-    send_out(1)
     for load in loads[4:]:
         load.wait()
     for copy in weights:
@@ -350,10 +359,6 @@
         def _():
             forward(i + 1)
 
-        @pl.when(i < 2)
-        def _():
-            send_out(i + 2)
-
         @pl.when(i < 4)
         def _():
             add_partner(i)
@@ -361,16 +366,20 @@
         @pl.when(jnp.logical_and(i >= 1, i < 5))
         def _():
             second_dots(i - 1)
+
+        @pl.when(i >= 2)
+        def _():
+            add_twin(i - 2, 0)
+
+        @pl.when(i >= 2)
+        def _():
+            add_twin(i - 2, 1)
 
         @pl.when(i == 4)
         def _():
             weight_grads(other)
             for copy in grads_away:
                 copy.start()
-
-        @pl.when(i >= 2)
-        def _():
-            add_twin(i - 2)
 
     loop(6, turn_of)
     weight_grads(role)

time: 147 us -> 136 us (0.925)
  the two profiles are of different devices: /device:TPU:67 before, /device:TPU:33 now
where the time goes in v4:
time: 136 us
  Pallas kernels  135 us (99%)
    pallas_call x1, Pallas kernels, per_device(): pl.pallas_call(kernel, out_shape=(jax.ShapeDtypeStruct((NY, 8) + piece, B...  130 us
    pallas_call x1, Pallas kernels, per_device(): pl.pallas_call(finish, out_shape=(jax.ShapeDtypeStruct((tok_count, width)...  5.25 us

profile of v4, /device:TPU:33, one launch (start us, length us, event | category | flops | bytes accessed | tf_op | source)
XLA Modules:
  0.0 136.0 jit_solution(10496645720309068327)
XLA Ops:
  0.6 130.1 %shard_map.110 = (bf16[4,8,2,8,1792]{4,3,2,1,0:T(8,128)(2,1)}, bf16[3584,128]{1,0:T(8,128)(2,1)}, bf16[3584,128]{1,0:T(8,128)(2,1)}, bf16[128,3584]{1,0:T(8,128)(2,1)}) custom-call(bf16[128,7168]{1,0:T(8,128)(2,1)} %tok_hbm.1, bf16[128,7168]{1,0:T(8,128)(2,1)} %cot_hbm.1, s32[8,128]{1,0:T(8,128)} %bitcast.11, f32[8,128]{1,0:T(8,128)} %bitcast.13, ...), custom_call_target="tpu_custom_call" | custom-call | tf_op jit(solution)/shard_map/pallas_call | solution.py:477
  130.8 5.2 %shard_map.111 = (bf16[128,7168]{1,0:T(8,128)(2,1)}, bf16[128,7168]{1,0:T(8,128)(2,1)}, bf16[3584,128]{1,0:T(8,128)(2,1)}, bf16[3584,128]{1,0:T(8,128)(2,1)}, bf16[128,3584]{1,0:T(8,128)(2,1)}) custom-call(s32[8,128]{1,0:T(8,128)} %bitcast.12, f32[8,128]{1,0:T(8,128)} %bitcast.14, bf16[4,8,2,8,1792]{4,3,2,1,0:T(8,128)(2,1)} %get-tuple-element.14.fb_hbm, ...), custom_call_target="tpu_custom_call" | custom-call | tf_op jit(solution)/shard_map/pallas_call | solution.py:540

commit v5 on v4

--- a/solution.py
+++ b/solution.py
@@ -339,12 +339,15 @@
     for copy in weights:
         copy.wait_recv()
 
-    def turn(ct):
+    def turn_down(ct):
+        cols = span(ct * NARROW, NARROW)
+        wdT[cols, :] = wd[:, cols].T
+
+    def turn_cat(ct):
         cols = span(ct * NARROW, NARROW)
         wcatT[:, cols] = wcat[cols, :].T
-        wdT[cols, :] = wd[:, cols].T
-
-    loop(quarter // NARROW, turn)
+
+    loop(quarter // NARROW, turn_down)
 
     def turn_of(i):
         @pl.when(i < 4)
@@ -355,6 +358,10 @@
         def _():
             activate(i - 1)
 
+        @pl.when(i == 0)
+        def _():
+            loop(quarter // NARROW, turn_cat)
+
         @pl.when(i < 3)
         def _():
             forward(i + 1)
@@ -369,11 +376,11 @@
 
         @pl.when(i >= 2)
         def _():
+            add_twin(i - 2, 1)
+
+        @pl.when(i >= 2)
+        def _():
             add_twin(i - 2, 0)
-
-        @pl.when(i >= 2)
-        def _():
-            add_twin(i - 2, 1)
 
         @pl.when(i == 4)
         def _():

time: 136 us -> 137 us (level)
  no operation moved by 1% of the time
where the time goes in v5:
time: 137 us; the launch traced here: 136 us
  Pallas kernels  135 us (99%)
    pallas_call x1, Pallas kernels, per_device(): pl.pallas_call(kernel, out_shape=(jax.ShapeDtypeStruct((NY, 8) + piece, B...  130 us
    pallas_call x1, Pallas kernels, per_device(): pl.pallas_call(finish, out_shape=(jax.ShapeDtypeStruct((tok_count, width)...  5.25 us

profile of v5, /device:TPU:33, one launch (start us, length us, event | category | flops | bytes accessed | tf_op | source)
XLA Modules:
  0.0 135.8 jit_solution(12634633768956500736)
XLA Ops:
  0.6 129.9 %shard_map.110 = (bf16[4,8,2,8,1792]{4,3,2,1,0:T(8,128)(2,1)}, bf16[3584,128]{1,0:T(8,128)(2,1)}, bf16[3584,128]{1,0:T(8,128)(2,1)}, bf16[128,3584]{1,0:T(8,128)(2,1)}) custom-call(bf16[128,7168]{1,0:T(8,128)(2,1)} %tok_hbm.1, bf16[128,7168]{1,0:T(8,128)(2,1)} %cot_hbm.1, s32[8,128]{1,0:T(8,128)} %bitcast.11, f32[8,128]{1,0:T(8,128)} %bitcast.13, ...), custom_call_target="tpu_custom_call" | custom-call | tf_op jit(solution)/shard_map/pallas_call | solution.py:484
  130.6 5.2 %shard_map.111 = (bf16[128,7168]{1,0:T(8,128)(2,1)}, bf16[128,7168]{1,0:T(8,128)(2,1)}, bf16[3584,128]{1,0:T(8,128)(2,1)}, bf16[3584,128]{1,0:T(8,128)(2,1)}, bf16[128,3584]{1,0:T(8,128)(2,1)}) custom-call(s32[8,128]{1,0:T(8,128)} %bitcast.12, f32[8,128]{1,0:T(8,128)} %bitcast.14, bf16[4,8,2,8,1792]{4,3,2,1,0:T(8,128)(2,1)} %get-tuple-element.14.fb_hbm, ...), custom_call_target="tpu_custom_call" | custom-call | tf_op jit(solution)/shard_map/pallas_call | solution.py:547
